TPU v7x, 128 devices: a whole 4x4x4 slice. The times are simulated.
128 devices in a mesh: dp: 4 (over y_hi, core), mp: 32 (over y_lo, x, z).
Axes of the slice: x: 4, y: 4 (y_hi: 2, y_lo: 2; y = y_hi * 2 + y_lo), z: 4, core: 2. Of those that a mesh axis runs over, the one named last changes fastest.
Arguments:
- tokens: bfloat16 [2048, 6144], P(('dp', 'mp')), may hold values from -6 to 6
- norm_gain: float32 [6144], replicated, may hold values from 0.1 to 1.9
- qkv_weight: bfloat16 [6144, 3, 4096], P(None, None, 'mp'), may hold values from -0.078125 to 0.078125
- up_weight: bfloat16 [6144, 12288], P(None, 'mp'), may hold values from -0.078125 to 0.078125
- proj_weight: bfloat16 [4096, 6144], P('mp'), may hold values from -0.09375 to 0.09375
- down_weight: bfloat16 [12288, 6144], P('mp'), may hold values from -0.0546875 to 0.0546875
- query_gain: float32 [128], replicated, may hold values from 0.1 to 1.9
- key_gain: float32 [128], replicated, may hold values from 0.1 to 1.9
- out_grad: bfloat16 [2048, 6144], P(('dp', 'mp')), may hold values from -6 to 6
Outputs:
- token_grad: bfloat16 [2048, 6144], P(('dp', 'mp'))
- norm_gain_grad: float32 [6144], replicated
- qk_gain_grad: float32 [2, 128], replicated
- qkv_grad: float32 [6144, 3, 4096], P('dp', None, 'mp')
- up_grad: float32 [6144, 12288], P('dp', 'mp')
- proj_grad: float32 [4096, 6144], P('mp', 'dp')
- down_grad: float32 [12288, 6144], P('mp', 'dp')
All inputs are finite; a program needn't handle non-finite values.
Results may differ from a plain program's by a relative error of at most 0.033.
Values may be sent and summed in bfloat16 or wider, within the bound.
A program may use at most 192 MiB of HBM per device.

v0:
```python
import jax
import jax.numpy as jnp
from jax import lax
from jax.sharding import PartitionSpec as P

HEAD_DIM = 128
PATCHES = 256


def head_norm(hidden, gain):
    factor = lax.rsqrt(jnp.mean(hidden * hidden, axis=-1, keepdims=True) + 1e-06)
    return (hidden * factor * gain).astype(jnp.bfloat16)


def row_scale(rows_float):
    return lax.rsqrt(jnp.mean(rows_float * rows_float, axis=1, keepdims=True) + 1e-06)


def attend_mix(hidden_qkv, hidden_up, query_gain, key_gain):
    row_count = hidden_qkv.shape[0]
    head_count = hidden_qkv.shape[2]
    head_size = hidden_qkv.shape[3]
    grid_shape = (row_count // PATCHES, PATCHES, head_count, head_size)
    queries = head_norm(hidden_qkv[:, 0], query_gain).reshape(grid_shape)
    keys_normed = head_norm(hidden_qkv[:, 1], key_gain).reshape(grid_shape)
    values_cast = hidden_qkv[:, 2].astype(jnp.bfloat16).reshape(grid_shape)
    scores = jnp.einsum(
        "ithe,ishe->ihts", queries, keys_normed, preferred_element_type=jnp.float32
    ) * head_size ** (-0.5)
    weights = jnp.exp(scores)
    probs = (weights / jnp.sum(weights, axis=-1, keepdims=True)).astype(jnp.bfloat16)
    attended = jnp.einsum("ihts,ishe->ithe", probs, values_cast, preferred_element_type=jnp.float32)
    attended = attended.reshape(row_count, head_count * head_size).astype(jnp.bfloat16)
    activated = jax.nn.gelu(hidden_up, approximate=True).astype(jnp.bfloat16)
    return (attended, activated)


def contract_last(left, right):
    return lax.dot_general(
        left, right, (((1,), (1,)), ((), ())), preferred_element_type=jnp.float32
    )


def contract_first(left, right):
    return lax.dot_general(
        left, right, (((0,), (0,)), ((), ())), preferred_element_type=jnp.float32
    )


def per_device(
    tokens,
    norm_gain,
    qkv_weight,
    up_weight,
    proj_weight,
    down_weight,
    query_gain,
    key_gain,
    out_grad,
):
    model_dim = tokens.shape[1]
    own_float = tokens.astype(jnp.float32)
    own_scale = row_scale(own_float)
    gathered = lax.all_gather(tokens, "mp", axis=0, tiled=True)
    gathered_float = gathered.astype(jnp.float32)
    normed = (gathered_float * row_scale(gathered_float) * norm_gain).astype(jnp.bfloat16)
    row_count = normed.shape[0]
    qkv_flat = qkv_weight.reshape(model_dim, -1)
    width_qkv = qkv_flat.shape[1]
    hidden_qkv = jnp.dot(normed, qkv_flat, preferred_element_type=jnp.float32).reshape(
        row_count, 3, -1, HEAD_DIM
    )
    hidden_up = jnp.dot(normed, up_weight, preferred_element_type=jnp.float32)
    (attended, activated), pullback = jax.vjp(
        attend_mix, hidden_qkv, hidden_up, query_gain, key_gain
    )
    cotangent = lax.all_gather(out_grad, "mp", axis=0, tiled=True)
    attended_grad = contract_last(cotangent, proj_weight).astype(jnp.bfloat16)
    activated_grad = contract_last(cotangent, down_weight).astype(jnp.bfloat16)
    qkv_cot, up_cot, query_cot, key_cot = pullback((attended_grad, activated_grad))
    hidden_grad = jnp.concatenate([qkv_cot.reshape(row_count, width_qkv), up_cot], axis=1).astype(
        jnp.bfloat16
    )
    normed_grad = lax.psum_scatter(
        (
            contract_last(hidden_grad[:, :width_qkv], qkv_flat)
            + contract_last(hidden_grad[:, width_qkv:], up_weight)
        ).astype(jnp.bfloat16),
        "mp",
        scatter_dimension=0,
        tiled=True,
    ).astype(jnp.float32)
    scaled = normed_grad * norm_gain
    inner_mean = jnp.mean(scaled * own_float, axis=1, keepdims=True)
    token_grad = (
        out_grad.astype(jnp.float32)
        + own_scale * scaled
        - own_float * own_scale * own_scale * own_scale * inner_mean
    ).astype(jnp.bfloat16)
    gain_term = jnp.sum(normed_grad * own_float * own_scale, axis=0)
    norm_gain_grad, qk_gain_grad = lax.psum(
        (gain_term, jnp.stack([query_cot, key_cot])), ("dp", "mp")
    )
    active = jnp.concatenate([attended, activated], axis=1)
    part_rows = model_dim // lax.axis_size("dp")
    summed = lax.psum_scatter(
        jnp.concatenate(
            [contract_first(normed, hidden_grad), contract_first(cotangent, active)], axis=1
        ).astype(jnp.bfloat16),
        "dp",
        scatter_dimension=0,
        tiled=True,
    ).astype(jnp.float32)
    in_cols = hidden_grad.shape[1]
    width_attn = proj_weight.shape[0]
    qkv_grad = summed[:, :width_qkv].reshape(part_rows, 3, -1)
    up_grad = summed[:, width_qkv:in_cols]
    proj_grad = summed[:, in_cols : in_cols + width_attn].T
    down_grad = summed[:, in_cols + width_attn :].T
    return (token_grad, norm_gain_grad, qk_gain_grad, qkv_grad, up_grad, proj_grad, down_grad)


def solution(mesh):
    placed = (
        P(("dp", "mp"), None),
        P(),
        P(None, None, "mp"),
        P(None, "mp"),
        P("mp", None),
        P("mp", None),
        P(),
        P(),
        P(("dp", "mp"), None),
    )
    return jax.shard_map(
        per_device,
        mesh=mesh,
        in_specs=placed,
        out_specs=(
            P(("dp", "mp"), None),
            P(),
            P(),
            P("dp", None, "mp"),
            P("dp", "mp"),
            P("mp", "dp"),
            P("mp", "dp"),
        ),
        check_vma=False,
    )
```

profile of v0, /device:TPU:10, one launch (start us, length us, event | category | flops | bytes accessed | tf_op | source)
XLA Modules:
  0.0 700.9 jit_solution(14575723502876432049)
XLA Ops:
  8.7 6.7 copy.26
  15.4 153.5 %all-gather.5.cloned.1.call-done = bf16[512,6144]{1,0:T(8,128)(2,1)} async-done(((bf16[16,6144]{1,0:T(8,128)(2,1)}), bf16[512,6144]{1,0:T(8,128)(2,1)}) %all-gather.5.cloned.1.call-update) | async-done | bytes 6291472 | tf_op jit(solution)/shard_map/all_gather | solution.py:64
  168.9 4.2 fusion
  173.2 5.6 fusion.7
  180.4 1.1 fusion.63
  182.6 151.9 %all-gather.3.cloned.1.call-done = bf16[512,6144]{1,0:T(8,128)(2,1)} async-done(((bf16[16,6144]{1,0:T(8,128)(2,1)}), bf16[512,6144]{1,0:T(8,128)(2,1)}) %all-gather.3.cloned.1.call-update) | async-done | bytes 6291472 | tf_op jit(solution)/shard_map/all_gather | solution.py:77
  334.5 5.2 convolution_convert_fusion.8
  345.3 9.2 %fusion.64 = f32[512,6144]{1,0:T(8,128)} fusion(bf16[512,384]{0,1:T(8,128)(2,1)S(1)} %bitcast.107, bf16[6144,384]{0,1:T(8,128)(2,1)} %bitcast.101), kind=kOutput, calls=%fused_computation.107 | convolution fusion | flops 2415919104 | bytes 17694720 | tf_op jit(solution)/shard_map/dot_general | solution.py:39
  354.5 6.7 multiply_convert_fusion
  361.2 3.0 fusion.25
  364.2 8.2 %add_convert_fusion = bf16[512,6144]{1,0:T(8,128)(2,1)} fusion(f32[512,6144]{1,0:T(8,128)} %fusion.64, bf16[512,384]{0,1:T(8,128)(2,1)S(1)} %fusion.25, bf16[6144,384]{1,0:T(8,128)(2,1)S(1)} %bitcast.106), kind=kOutput, calls=%fused_computation.6 | convolution fusion | flops 2422210560 | bytes 23986176 | tf_op jit(solution)/shard_map/dot_general | solution.py:39
  372.9 6.8 fusion.3
  379.8 5.5 convolution_convert_fusion
  385.3 6.9 pad_maximum_fusion
  393.4 152.2 %reduce-scatter.3.cloned.1.call-done = bf16[16,6144]{1,0:T(8,128)(2,1)} async-done(((bf16[512,6144]{1,0:T(8,128)(2,1)}), bf16[16,6144]{1,0:T(8,128)(2,1)}) %reduce-scatter.3.cloned.1.call-update) | async-done | bytes 196624 | tf_op jit(solution)/shard_map/reduce_scatter | solution.py:84
  545.6 1.2 fusion.42
  546.8 76.6 %all-reduce.3 = (f32[6144]{0:T(1024)}, f32[2,128]{1,0:T(2,128)}) all-reduce(f32[6144]{0:T(1024)S(1)} %get-tuple-element.29, f32[2,128]{1,0:T(2,128)S(1)} %pad_maximum_fusion.1), channel_id=1, replica_groups=mesh['dp'=4,'mp'=32] {'dp','mp'}, use_global_device_ids=true, to_apply=%region_11.0 | all-reduce | flops 6400 | bytes 51200 | tf_op jit(solution)/shard_map/psum | solution.py:101
  623.4 1.8 fusion.35
  625.2 54.3 %reduce-scatter.5.cloned.1.call-done = bf16[1536,1280]{0,1:T(8,128)(2,1)} async-done(((bf16[6144,1280]{0,1:T(8,128)(2,1)}), bf16[1536,1280]{0,1:T(8,128)(2,1)}) %reduce-scatter.5.cloned.1.call-update) | async-done | bytes 3932176 | tf_op jit(solution)/shard_map/reduce_scatter | solution.py:106
  679.5 3.4 convert_element_type.217
  683.8 1.6 slice_bitcast_fusion
  685.4 2.8 fusion.61
  688.2 3.0 copy.34
  691.3 3.0 copy.35
  (85 shorter events, 12.1 us)
Async XLA Ops:
  7.2 327.3 %copy-start = (bf16[128,6144]{1,0:T(8,128)(2,1)S(1)}, bf16[128,6144]{1,0:T(8,128)(2,1)}, u32[]{:S(2)}) copy-start(bf16[128,6144]{1,0:T(8,128)(2,1)} %param.13) | copy-start | bytes 4718596
  7.2 161.7 %all-gather.5.cloned.1.call-start = ((), (), s32[]{:S(2)}) async-start(), calls=%async_computation.3 | async-start | bytes 6488064 | tf_op jit(solution)/shard_map/all_gather | solution.py:64
  7.9 326.6 %all-gather.3.cloned.1.call-start = ((), (), s32[]{:S(2)}) async-start(), calls=%async_computation.2 | async-start | bytes 6488064 | tf_op jit(solution)/shard_map/all_gather | solution.py:77
  8.7 164.5 %copy-start.6 = (f32[6144]{0:T(1024)S(1)}, f32[6144]{0:T(1024)}, u32[]{:S(2)}) copy-start(f32[6144]{0:T(1024)} %param.10) | copy-start | bytes 73732
  8.7 536.9 %reduce-scatter.3.cloned.1.call-start = ((), (), s32[]{:S(2)}) async-start(), calls=%async_computation.4 | async-start | bytes 6488064 | tf_op jit(solution)/shard_map/reduce_scatter | solution.py:84
  168.9 4.3 copy-start.3
  173.2 5.7 copy-start.12
  339.7 4.1 copy-start.9
  339.7 4.5 copy-start.10
  339.7 4.5 copy-start.11
  345.0 9.5 %slice-start.2 = ((s8[4718592]{0:T(1024)(128)(4,1)}), s8[524288]{0:T(1024)(128)(4,1)S(1)}, s32[]{:S(2)}) async-start(s8[4718592]{0:T(1024)(128)(4,1)} %bitcast.105), calls=%async_computation.8 | async-start | bytes 1048576
  345.2 9.2 %slice-start.3 = ((s8[4718592]{0:T(1024)(128)(4,1)}), s8[4194304]{0:T(1024)(128)(4,1)S(1)}, s32[]{:S(2)}) async-start(s8[4718592]{0:T(1024)(128)(4,1)} %bitcast.105), calls=%async_computation.9 | async-start | bytes 8388608
  345.3 9.2 %copy-start.7 = (f32[6144]{0:T(1024)S(1)}, f32[6144]{0:T(1024)}, u32[]{:S(2)}) copy-start(f32[6144]{0:T(1024)} %param.10) | copy-start | bytes 73732
  345.3 9.2 %copy-start.13 = (f32[512]{0:T(512)S(1)}, f32[512]{0:T(512)}, u32[]{:S(2)}) copy-start(f32[512]{0:T(512)} %copy-done.12) | copy-start | bytes 6148
  345.3 15.9 %slice-start.4 = ((s8[6291456]{0:T(1024)(128)(4,1)}), s8[4194304]{0:T(1024)(128)(4,1)S(1)}, s32[]{:S(2)}) async-start(s8[6291456]{0:T(1024)(128)(4,1)} %bitcast.123), calls=%async_computation.10 | async-start | bytes 8388608
  345.3 15.9 %slice-start.6 = ((s8[4718592]{0:T(1024)(128)(4,1)}), s8[4194304]{0:T(1024)(128)(4,1)S(1)}, s32[]{:S(2)}) async-start(s8[4718592]{0:T(1024)(128)(4,1)} %bitcast.125), calls=%async_computation.12 | async-start | bytes 8388608
  354.5 6.7 slice-start.5
  354.5 6.7 slice-start.7
  372.5 307.1 %reduce-scatter.5.cloned.1.call-start = ((), (), s32[]{:S(2)}) async-start(), calls=%async_computation.5 | async-start | bytes 19660800 | tf_op jit(solution)/shard_map/reduce_scatter | solution.py:106
  372.5 7.3 %slice-start = ((s8[6291456]{0:T(1024)(128)(4,1)}), s8[4194304]{0:T(1024)(128)(4,1)S(1)}, s32[]{:S(2)}) async-start(s8[6291456]{0:T(1024)(128)(4,1)} %bitcast.103), calls=%async_computation.6 | async-start | bytes 8388608
  372.9 6.9 slice-start.1
  392.2 231.2 %copy-start.5 = (bf16[16,6144]{1,0:T(8,128)(2,1)S(1)}, bf16[16,6144]{1,0:T(8,128)(2,1)}, u32[]{:S(2)}) copy-start(bf16[16,6144]{1,0:T(8,128)(2,1)} %param.17) | copy-start | bytes 589828
  679.5 5.9 copy-start.2
  685.4 8.9 %copy-start.1 = (bf16[128,6144]{1,0:T(8,128)(2,1)S(1)}, bf16[128,6144]{1,0:T(8,128)(2,1)}, u32[]{:S(2)}) copy-start(bf16[128,6144]{1,0:T(8,128)(2,1)} %param.13) | copy-start | bytes 4718596
  (2 other events, 1.5 us)
Sparse Core Ops, SparseCore 0:
  9.7 159.2 all-gather.4
  170.6 163.8 all-gather.2
  372.6 172.9 reduce-scatter.2
  548.1 131.3 reduce-scatter.4
where the time goes:
time: 705 us; the launch traced here: 701 us
  waiting for transfers between devices  513 us (73%)
  blocking collectives  76.6 us (11%)
  matrix products  54.8 us (8%)
  local copies, waits for them, and re-layouts  22.4 us (3%)
  other arithmetic  19.3 us (3%)
  between operations  14.2 us (2%)
    all_gather x1, waiting for transfers between devices, per_device(): gathered = lax.all_gather(tokens, 'mp', axis=0, tiled=True)  153 us
    reduce_scatter x1, waiting for transfers between devices, per_device(): lax.psum_scatter((contract_last(hidden_grad[:, :width_qkv], qkv_flat) + c...  152 us
    all_gather x1, waiting for transfers between devices, per_device(): cotangent = lax.all_gather(out_grad, 'mp', axis=0, tiled=True)  152 us
    psum x1, blocking collectives, per_device(): lax.psum((gain_term, jnp.stack([query_cot, key_cot])), ('dp', 'mp'))  76.6 us
    reduce_scatter x1, waiting for transfers between devices, per_device(): lax.psum_scatter(jnp.concatenate([contract_first(normed, hidden_grad), co...  54.3 us
    dot_general x4, matrix products, contract_last(): lax.dot_general(left, right, (((1,), (1,)), ((), ())), preferred_element_...  25.6 us
    unnamed x48, local copies, waits for them, and re-layouts  14.4 us
  transfers between devices with their start and end apart: 4, of which 4 were waited for; matrix products, arithmetic and copies ran while one was open for 6% of the time, Pallas kernels for 0%

commit v1 on v0

v1 whole, which is shorter than its diff:
```python
import jax
import jax.numpy as jnp
from jax import lax
from jax.experimental import pallas as pl
from jax.experimental.pallas import tpu as pltpu
from jax.sharding import PartitionSpec as P

F32, BF16 = jnp.float32, jnp.bfloat16
MESH = pl.DeviceIdType.MESH

D = 6144
HALF = D // 2
QUART = D // 4
PATCHES = 256
HEAD = 128
UP = 384
W_IN = 3 * HEAD + UP
W_OUT = HEAD + UP
ROWS = 16
TILE = 256
PART = (slice(0, HALF // 2), slice(HALF // 2, HALF))
EPS = 1e-06
GELU_A, GELU_B = 0.7978845608028654, 0.044715


def dot(left, right, dims):
    return lax.dot_general(left, right, (dims, ((), ())), preferred_element_type=F32)


def kernel(
    tok_ref, og_ref, gain_ref, qg_ref, kg_ref, wqkv_ref, wup_ref, wproj_ref, wdown_ref,
    tg_ref, gsum_ref, dqkv_ref, dup_ref, dout_ref,
    nrm, N, C, G, win, wout, XS, XR, H, HG, ACT, FB1, MB1, FB2, MB2, FS, MS, YR,
    SD, RD, SO, RO, GS, GQ, GC, GY, GX, GZ,
    wsem, y_s, y_r, ag_s, ag_r, e_s, e_r, rs_s, rs_r, z_s, z_r, d_s, d_r, g_s, g_r,
):
    dp, mp = lax.axis_index("dp"), lax.axis_index("mp")
    y_hi, core = dp // 2, dp % 2
    y_lo, x, z = mp // 16, (mp // 4) % 4, mp % 4
    y = y_hi * 2 + y_lo

    def dev(dx=0, dy=0, dz=0, dc=0):
        xx, yy, zz, cc = (x + dx) % 4, (y + dy) % 4, (z + dz) % 4, (core + dc) % 2
        return ((yy // 2) * 2 + cc, (yy % 2) * 16 + xx * 4 + zz)

    def copy(src, dst, send, recv, to):
        return pltpu.make_async_remote_copy(
            src_ref=src, dst_ref=dst, send_sem=send, recv_sem=recv, device_id=to, device_id_type=MESH
        )

    pending = []

    def send(*args):
        cp = copy(*args)
        cp.start()
        pending.append(cp)
        return cp

    half = pl.ds(pl.multiple_of(y_hi * HALF, HALF), HALF)
    loads = [
        pltpu.make_async_copy(wqkv_ref.at[j, half], win.at[:, pl.ds(j * HEAD, HEAD)], wsem.at[j])
        for j in range(3)
    ]
    loads.append(pltpu.make_async_copy(wup_ref.at[half], win.at[:, pl.ds(3 * HEAD, UP)], wsem.at[3]))
    loads.append(pltpu.make_async_copy(wproj_ref.at[:, half], wout.at[pl.ds(0, HEAD)], wsem.at[4]))
    loads.append(pltpu.make_async_copy(wdown_ref.at[:, half], wout.at[pl.ds(HEAD, UP)], wsem.at[5]))
    for cp in loads:
        cp.start()

    barrier = pltpu.get_barrier_semaphore()
    peers = [dev(dy=d) for d in (1, 2, 3)] + [dev(dx=d) for d in (1, 2, 3)]
    peers += [dev(dz=d) for d in (1, 2, 3)] + [dev(dc=1)]
    for peer in peers:
        pl.semaphore_signal(barrier, inc=1, device_id=peer, device_id_type=MESH)

    tok = tok_ref[...].astype(F32)
    scale = lax.rsqrt(jnp.mean(tok * tok, axis=1, keepdims=True) + EPS)
    nrm[...] = (tok * scale * gain_ref[...]).astype(BF16)
    zrow = pl.ds(pl.multiple_of(z * ROWS, ROWS), ROWS)
    N[y_lo, y_hi, x, zrow, :] = nrm[:, half]
    C[y_lo, y_hi, x, zrow, :] = og_ref[:, half]
    GS[...] = jnp.zeros_like(GS)
    GQ[...] = jnp.zeros_like(GQ)
    pl.semaphore_wait(barrier, len(peers))

    y_copies = []
    for a, (src, dst) in enumerate(((nrm, N), (og_ref, C))):
        row = []
        for dy in (1, 2, 3):
            there = ((y + dy) % 4) // 2
            cols = pl.ds(pl.multiple_of(there * HALF, HALF), HALF)
            row.append(
                send(src.at[:, cols], dst.at[y_lo, y_hi, x, zrow, :],
                     y_s.at[a, dy - 1], y_r.at[a, dy - 1], dev(dy=dy))
            )
        y_copies.append(row)

    def zr(i):
        return pl.ds(pl.multiple_of(((z + i) % 4) * ROWS, ROWS), ROWS)

    def ag_first(ref, k, p, off, yh):
        if p == 0:
            return ref.at[k, yh, (x + off) % 4, zrow, PART[0]]
        return ref.at[k, yh, x, zr(off), PART[1]]

    def ag_second(ref, k, p, off, yh):
        if p == 0:
            return ref.at[k, yh, :, zr(off), PART[0]]
        return ref.at[k, yh, (x + off) % 4, :, PART[1]]

    def ag_dev(p, phase, step):
        return dev(dx=step) if p == phase else dev(dz=step)

    units = [(N, 0), (C, 0), (N, 1), (C, 1)]
    ag = {}

    def ag_own(u, phase):
        ref, k = units[u]
        where = (ag_first, ag_second)[phase]
        for p in (0, 1):
            for d, step in enumerate((1, -1)):
                block = where(ref, k, p, 0, slice(None))
                ag[u, phase, 0, p, d] = send(
                    block, block, ag_s.at[u, phase, p, d], ag_r.at[u, phase, p, d], ag_dev(p, phase, step)
                )

    def ag_fwd(u, phase):
        ref, k = units[u]
        where = (ag_first, ag_second)[phase]
        for p in (0, 1):
            for d, step in enumerate((1, -1)):
                ag[u, phase, 0, p, d].wait_recv()
                block = where(ref, k, p, -step, d)
                ag[u, phase, 1, p, d] = send(
                    block, block, ag_s.at[u, phase, p, 2 + d], ag_r.at[u, phase, p, 2 + d],
                    ag_dev(p, phase, step),
                )

    def ag_end(u, phase):
        for p in (0, 1):
            for d in (0, 1):
                ag[u, phase, 1, p, d].wait_recv()

    partner = dev(dy=2)

    def rows_of(ref, k, yh):
        return ref[k, yh].reshape(PATCHES, HALF)

    def partial_in(k):
        other = 1 - y_hi

        @pl.loop(0, W_IN // TILE)
        def _(j):
            cols = pl.ds(pl.multiple_of(j * TILE, TILE), TILE)
            XS[k, :, cols] = dot(rows_of(N, k, other), win[:, cols], ((1,), (0,))).astype(BF16)

        cp = send(XS.at[k, :, pl.ds(0, W_IN)], XR.at[k, :, pl.ds(0, W_IN)], e_s.at[k, 0], e_r.at[k, 0], partner)

        @pl.loop(0, W_IN // TILE)
        def _(j):
            cols = pl.ds(pl.multiple_of(j * TILE, TILE), TILE)
            H[k, :, cols] = dot(rows_of(N, k, y_hi), win[:, cols], ((1,), (0,)))

        return cp

    def partial_out(k):
        other = 1 - y_hi

        @pl.loop(0, W_OUT // TILE)
        def _(j):
            rows = pl.ds(pl.multiple_of(j * TILE, TILE), TILE)
            cols = pl.ds(pl.multiple_of(W_IN + j * TILE, TILE), TILE)
            XS[k, :, cols] = dot(rows_of(C, k, other), wout[rows, :], ((1,), (1,))).astype(BF16)

        cp = send(XS.at[k, :, pl.ds(W_IN, W_OUT)], XR.at[k, :, pl.ds(W_IN, W_OUT)],
                  e_s.at[k, 1], e_r.at[k, 1], partner)

        @pl.loop(0, W_OUT // TILE)
        def _(j):
            rows = pl.ds(pl.multiple_of(j * TILE, TILE), TILE)
            cols = pl.ds(pl.multiple_of(W_IN + j * TILE, TILE), TILE)
            H[k, :, cols] = dot(rows_of(C, k, y_hi), wout[rows, :], ((1,), (1,)))

        return cp

    def summed(k, start, width, rows=slice(None)):
        cols = pl.ds(start, width)
        return H[k, rows, cols] + XR[k, rows, cols].astype(F32)

    def head_norm(h, g):
        factor = lax.rsqrt(jnp.mean(h * h, axis=1, keepdims=True) + EPS)
        return factor, (h * factor * g).astype(BF16)

    def head_norm_back(h, factor, g, dy):
        hf = h * factor
        dyg = dy * g
        dh = factor * (dyg - hf * jnp.mean(hf * dyg, axis=1, keepdims=True))
        return dh, jnp.sum(dy * hf, axis=0, keepdims=True)

    def middle(k):
        hq, hk = summed(k, 0, HEAD), summed(k, HEAD, HEAD)
        v = summed(k, 2 * HEAD, HEAD).astype(BF16)
        da = summed(k, W_IN, HEAD).astype(BF16)
        qg, kg = qg_ref[...], kg_ref[...]
        fq, qn = head_norm(hq, qg)
        fk, kn = head_norm(hk, kg)
        w = jnp.exp(dot(qn, kn, ((1,), (1,))) * HEAD**-0.5)
        probs = w / jnp.sum(w, axis=1, keepdims=True)
        probs_b = probs.astype(BF16)
        ACT[k, y_hi, :, 0:HEAD] = dot(probs_b, v, ((1,), (0,))).astype(BF16)
        dpr = dot(da, v, ((1,), (1,))).astype(BF16).astype(F32)
        HG[k, y_hi, :, 2 * HEAD : 3 * HEAD] = dot(probs_b, da, ((0,), (0,))).astype(BF16)
        ds = probs * (dpr - jnp.sum(probs * dpr, axis=1, keepdims=True))
        ds = (ds * HEAD**-0.5).astype(BF16)
        dqn = dot(ds, kn, ((1,), (0,))).astype(BF16).astype(F32)
        dkn = dot(ds, qn, ((0,), (0,))).astype(BF16).astype(F32)
        dhq, dqg = head_norm_back(hq, fq, qg, dqn)
        dhk, dkg = head_norm_back(hk, fk, kg, dkn)
        HG[k, y_hi, :, 0:HEAD] = dhq.astype(BF16)
        HG[k, y_hi, :, HEAD : 2 * HEAD] = dhk.astype(BF16)
        GQ[0:1, :] += dqg
        GQ[1:2, :] += dkg

        @pl.loop(0, 4)
        def _(i):
            rows = pl.ds(pl.multiple_of(i * 64, 64), 64)
            u = summed(k, 3 * HEAD, UP, rows)
            dact = summed(k, W_IN + HEAD, UP, rows).astype(BF16).astype(F32)
            t = jnp.tanh(GELU_A * (u + GELU_B * (u * u * u)))
            ACT[k, y_hi, rows, HEAD:] = (0.5 * u * (1.0 + t)).astype(BF16)
            slope = 0.5 * (1.0 + t) + 0.5 * u * (1.0 - t * t) * (GELU_A * (1.0 + 3.0 * GELU_B * (u * u)))
            HG[k, y_hi, rows, 3 * HEAD :] = (dact * slope).astype(BF16)

        return (
            send(HG.at[k, y_hi], HG.at[k, y_hi], e_s.at[k, 2], e_r.at[k, 2], partner),
            send(ACT.at[k, y_hi], ACT.at[k, y_hi], e_s.at[k, 3], e_r.at[k, 3], partner),
        )

    def normed_grad(k, yh):
        @pl.loop(0, HALF // TILE)
        def _(j):
            cols = pl.ds(pl.multiple_of(j * TILE, TILE), TILE)
            ng = dot(HG[k, yh], win[cols, :], ((1,), (1,)))
            G[k, yh, :, :, cols] = ng.astype(BF16).reshape(4, 64, TILE)
            term = ng * N[k, yh, :, :, cols].reshape(PATCHES, TILE).astype(F32)
            GS[:, cols] += jnp.sum(term.reshape(PATCHES // 8, 8, TILE), axis=0)

    def rs_bufs(k, phase, p):
        if phase == 1:
            return (FB1, FB2)[p].at[k], (MB1, MB2)[p].at[k]
        return FS.at[p, k], MS.at[p, k]

    rs = {}

    def rs_start(k, phase):
        where = (ag_first, ag_second)[phase]
        for p in (0, 1):
            fr, mr = rs_bufs(k, phase, p)
            for d, step in enumerate((1, -1)):
                to = ag_dev(p, phase, step)
                sems = lambda i: (rs_s.at[k, phase, p, d, i], rs_r.at[k, phase, p, d, i])
                rs[k, phase, p, d, 0] = send(where(G, k, p, 2, d), fr.at[d], *sems(0), to)
                rs[k, phase, p, d, 1] = send(where(G, k, p, step, 1 - d), mr.at[d, 1 - d], *sems(1), to)

    def rs_mid(k, phase):
        where = (ag_first, ag_second)[phase]
        for p in (0, 1):
            fr, mr = rs_bufs(k, phase, p)
            for d, step in enumerate((1, -1)):
                to = ag_dev(p, phase, step)
                rs[k, phase, p, d, 0].wait_recv()
                block = where(G, k, p, step, d)
                block[...] = (block[...].astype(F32) + fr[d].astype(F32)).astype(BF16)
                rs[k, phase, p, d, 2] = send(
                    block, mr.at[d, d], rs_s.at[k, phase, p, d, 2], rs_r.at[k, phase, p, d, 2], to
                )

    def rs_end(k, phase):
        where = (ag_first, ag_second)[phase]
        for p in (0, 1):
            _, mr = rs_bufs(k, phase, p)
            for d in (0, 1):
                rs[k, phase, p, d, 1].wait_recv()
                rs[k, phase, p, d, 2].wait_recv()
            for yh in (0, 1):
                block = where(G, k, p, 0, yh)
                total = block[...].astype(F32) + mr[0, yh].astype(F32) + mr[1, yh].astype(F32)
                block[...] = total.astype(BF16)

    def feature_tile(t, whose):
        return pl.ds(pl.multiple_of(whose * QUART + t * TILE, TILE), TILE)

    def grad_in(t, whose):
        left = N[:, :, :, :, feature_tile(t, whose)].reshape(4 * PATCHES, TILE)
        return dot(left, HG[...].reshape(4 * PATCHES, W_IN), ((0,), (0,)))

    def grad_out(t, whose):
        right = C[:, :, :, :, feature_tile(t, whose)].reshape(4 * PATCHES, TILE)
        return dot(ACT[...].reshape(4 * PATCHES, W_OUT), right, ((0,), (0,)))

    def swap(kind, t):
        src, dst = ((SD, RD), (SO, RO))[kind]
        return copy(src.at[t], dst.at[t], d_s.at[kind, t], d_r.at[kind, t], dev(dc=1))

    tiles = QUART // TILE

    def grads_away():
        @pl.loop(0, tiles)
        def _(t):
            SD[t] = grad_in(t, 1 - core).astype(BF16)
            swap(0, t).start()

        @pl.loop(0, tiles)
        def _(t):
            SO[t] = grad_out(t, 1 - core).astype(BF16)
            swap(1, t).start()

    def grads_in_here():
        @pl.loop(0, tiles)
        def _(t):
            own = grad_in(t, core)
            swap(0, t).wait_recv()
            rows = pl.ds(pl.multiple_of(t * TILE, TILE), TILE)
            total = own + RD[t].astype(F32)
            for j in range(3):
                dqkv_ref[j, rows, :] = total[:, j * HEAD : (j + 1) * HEAD].astype(BF16)
            dup_ref[rows, :] = total[:, 3 * HEAD :].astype(BF16)

    def grads_out_here():
        @pl.loop(0, tiles)
        def _(t):
            own = grad_out(t, core)
            swap(1, t).wait_recv()
            cols = pl.ds(pl.multiple_of(t * TILE, TILE), TILE)
            dout_ref[:, cols] = (own + RO[t].astype(F32)).astype(BF16)

    def gain_send(stage, slots, me, tos):
        return [
            send(slots.at[me], slots.at[me], g_s.at[stage, i], g_r.at[stage, i], to)
            for i, to in enumerate(tos)
        ]

    def wait_all(cps):
        for cp in cps:
            cp.wait_recv()

    wait_all(y_copies[0])
    ag_own(0, 0)
    wait_all(y_copies[1])
    ag_own(1, 0)
    ag_fwd(0, 0)
    ag_end(0, 0)
    ag_own(0, 1)
    ag_fwd(1, 0)
    ag_end(1, 0)
    ag_own(1, 1)
    ag_own(2, 0)
    for cp in loads:
        cp.wait()
    ag_fwd(0, 1)
    ag_fwd(2, 0)
    ag_end(2, 0)
    ag_own(2, 1)
    ag_own(3, 0)
    ag_end(0, 1)
    e_in0 = partial_in(0)
    ag_fwd(1, 1)
    ag_fwd(3, 0)
    ag_end(3, 0)
    ag_own(3, 1)
    ag_end(1, 1)
    e_out0 = partial_out(0)
    ag_fwd(2, 1)
    wait_all((e_in0, e_out0))
    back0 = middle(0)
    ag_end(2, 1)
    e_in1 = partial_in(1)
    ag_fwd(3, 1)
    normed_grad(0, y_hi)
    wait_all(back0)
    normed_grad(0, 1 - y_hi)
    rs_start(0, 1)
    ag_end(3, 1)
    e_out1 = partial_out(1)
    rs_mid(0, 1)
    wait_all((e_in1, e_out1))
    back1 = middle(1)
    rs_end(0, 1)
    rs_start(0, 0)
    normed_grad(1, y_hi)
    rs_mid(0, 0)
    wait_all(back1)
    normed_grad(1, 1 - y_hi)
    rs_start(1, 1)
    rs_end(0, 0)
    gsum = jnp.sum(GS[...], axis=0, keepdims=True)
    for j in range(HALF // HEAD):
        GC[core, j : j + 1, :] = gsum[:, j * HEAD : (j + 1) * HEAD]
    GC[core, 24:32, :] = GQ[...]
    g0 = gain_send(0, GC, core, [dev(dc=1)])
    grads_away()
    rs_mid(1, 1)
    wait_all(g0)
    GY[y] = GC[0] + GC[1]
    g1 = gain_send(1, GY, y, [dev(dy=d) for d in (1, 2, 3)])
    grads_in_here()
    rs_end(1, 1)
    rs_start(1, 0)
    wait_all(g1)
    GX[x, 0] = GY[0] + GY[1]
    GX[x, 1] = GY[2] + GY[3]
    g2 = gain_send(2, GX, x, [dev(dx=d) for d in (1, 2, 3)])
    rs_mid(1, 0)
    grads_out_here()
    rs_end(1, 0)

    last = []
    for dy in (1, 2, 3):
        yy = (y + dy) % 4
        last.append(
            send(G.at[yy % 2, yy // 2, x, zrow, :], YR.at[y], z_s.at[dy - 1], z_r.at[dy - 1], dev(dy=dy))
        )
    YR[y] = G[y_lo, y_hi, x, zrow, :]
    wait_all(g2)
    GZ[z] = ((GX[0] + GX[1]) + GX[2]) + GX[3]
    g3 = gain_send(3, GZ, z, [dev(dz=d) for d in (1, 2, 3)])
    wait_all(last)
    inner = jnp.zeros((ROWS, 1), F32)
    for h in (0, 1):
        cols = slice(h * HALF, (h + 1) * HALF)
        c = (YR[2 * h].astype(F32) + YR[2 * h + 1].astype(F32)) * gain_ref[:, cols]
        inner += jnp.sum(c * tok_ref[:, cols].astype(F32), axis=1, keepdims=True)
    inner = inner / D
    for h in (0, 1):
        cols = slice(h * HALF, (h + 1) * HALF)
        c = (YR[2 * h].astype(F32) + YR[2 * h + 1].astype(F32)) * gain_ref[:, cols]
        own = tok_ref[:, cols].astype(F32)
        grad = og_ref[:, cols].astype(F32) + scale * c - own * (scale * scale * scale * inner)
        tg_ref[:, cols] = grad.astype(BF16)
    wait_all(g3)
    gsum_ref[...] = ((GZ[0] + GZ[1]) + GZ[2]) + GZ[3]

    for cp in pending:
        cp.wait_send()

    @pl.loop(0, tiles)
    def _(t):
        swap(0, t).wait_send()
        swap(1, t).wait_send()


def per_device(tokens, norm_gain, qkv_weight, up_weight, proj_weight, down_weight, query_gain, key_gain, out_grad):
    vm, hbm = pl.BlockSpec(memory_space=pltpu.VMEM), pl.BlockSpec(memory_space=pl.ANY)
    tiles = QUART // TILE
    quarter = HALF // 2
    dma = pltpu.SemaphoreType.DMA
    scratch = [
        pltpu.VMEM((ROWS, D), BF16),
        pltpu.VMEM((2, 2, 4, 64, HALF), BF16),
        pltpu.VMEM((2, 2, 4, 64, HALF), BF16),
        pltpu.VMEM((2, 2, 4, 64, HALF), BF16),
        pltpu.VMEM((HALF, W_IN), BF16),
        pltpu.VMEM((W_OUT, HALF), BF16),
        pltpu.VMEM((2, PATCHES, W_IN + W_OUT), BF16),
        pltpu.VMEM((2, PATCHES, W_IN + W_OUT), BF16),
        pltpu.VMEM((2, PATCHES, W_IN + W_OUT), F32),
        pltpu.VMEM((2, 2, PATCHES, W_IN), BF16),
        pltpu.VMEM((2, 2, PATCHES, W_OUT), BF16),
        pltpu.VMEM((2, 2, 4, ROWS, quarter), BF16),
        pltpu.VMEM((2, 2, 2, 4, ROWS, quarter), BF16),
        pltpu.VMEM((2, 2, 64, quarter), BF16),
        pltpu.VMEM((2, 2, 2, 64, quarter), BF16),
        pltpu.VMEM((2, 2, 2, ROWS, quarter), BF16),
        pltpu.VMEM((2, 2, 2, 2, ROWS, quarter), BF16),
        pltpu.VMEM((4, ROWS, HALF), BF16),
        pltpu.VMEM((tiles, TILE, W_IN), BF16),
        pltpu.VMEM((tiles, TILE, W_IN), BF16),
        pltpu.VMEM((tiles, W_OUT, TILE), BF16),
        pltpu.VMEM((tiles, W_OUT, TILE), BF16),
        pltpu.VMEM((8, HALF), F32),
        pltpu.VMEM((8, HEAD), F32),
        pltpu.VMEM((2, 32, HEAD), F32),
        pltpu.VMEM((4, 32, HEAD), F32),
        pltpu.VMEM((4, 2, 32, HEAD), F32),
        pltpu.VMEM((4, 2, 32, HEAD), F32),
        dma((6,)),
        dma((2, 3)),
        dma((2, 3)),
        dma((4, 2, 2, 4)),
        dma((4, 2, 2, 4)),
        dma((2, 4)),
        dma((2, 4)),
        dma((2, 2, 2, 2, 3)),
        dma((2, 2, 2, 2, 3)),
        dma((3,)),
        dma((3,)),
        dma((2, tiles)),
        dma((2, tiles)),
        dma((4, 3)),
        dma((4, 3)),
    ]
    token_grad, gains, dqkv, dup, dout = pl.pallas_call(
        kernel,
        name="block",
        out_shape=(
            jax.ShapeDtypeStruct((ROWS, D), BF16),
            jax.ShapeDtypeStruct((2, 32, HEAD), F32),
            jax.ShapeDtypeStruct((3, QUART, HEAD), BF16),
            jax.ShapeDtypeStruct((QUART, UP), BF16),
            jax.ShapeDtypeStruct((W_OUT, QUART), BF16),
        ),
        in_specs=[vm] * 5 + [hbm] * 4,
        out_specs=(vm,) * 5,
        scratch_shapes=scratch,
        compiler_params=pltpu.CompilerParams(
            collective_id=0, has_side_effects=True, vmem_limit_bytes=60 * 1024 * 1024
        ),
        cost_estimate=pl.CostEstimate(flops=21 * 10**9, bytes_accessed=20 * 10**6, transcendentals=0),
    )(
        tokens, out_grad, norm_gain.reshape(1, D), query_gain.reshape(1, HEAD), key_gain.reshape(1, HEAD),
        jnp.transpose(qkv_weight, (1, 0, 2)), up_weight, proj_weight, down_weight,
    )
    norm_gain_grad = gains[:, : HALF // HEAD].reshape(D) / norm_gain
    qk_gain_grad = gains[0, 24:26] + gains[1, 24:26]
    return (
        token_grad,
        norm_gain_grad,
        qk_gain_grad,
        jnp.transpose(dqkv, (1, 0, 2)).astype(F32),
        dup.astype(F32),
        dout[:HEAD].astype(F32),
        dout[HEAD:].astype(F32),
    )


def solution(mesh):
    rows = P(("dp", "mp"), None)
    placed = (rows, P(), P(None, None, "mp"), P(None, "mp"), P("mp", None), P("mp", None), P(), P(), rows)
    outs = (rows, P(), P(), P("dp", None, "mp"), P("dp", "mp"), P("mp", "dp"), P("mp", "dp"))
    return jax.shard_map(per_device, mesh=mesh, in_specs=placed, out_specs=outs, check_vma=False)
```

time: 705 us -> 171 us (0.24)
  waiting for transfers between devices: 513 us -> 0 us
  Pallas kernels: 0 us -> 157 us
  blocking collectives: 76.6 us -> 0 us
  matrix products: 54.8 us -> 0 us
  local copies, waits for them, and re-layouts: 22.4 us -> 1.59 us
  between operations: 14.2 us -> 0.66 us
  other arithmetic: 19.3 us -> 10 us
    all_gather x2 -> x0, waiting for transfers between devices: 305 us -> none  [the longest x1 153 us: per_device(): gathered = lax.all_gather(tokens, 'mp', axis=0, tiled=True)]
    reduce_scatter x2 -> x0, waiting for transfers between devices: 207 us -> none  [the longest x1 152 us: per_device(): lax.psum_scatter((contract_last(hidden_grad[:, :width_qkv], qkv_flat) + c...]
    pallas_call x0 -> x1, Pallas kernels: none -> 157 us  [per_device(): pl.pallas_call(kernel, name='block', out_shape=(jax.ShapeDtypeStruct((ROW...]
    psum x1 -> x0, blocking collectives: 76.6 us -> none  [per_device(): lax.psum((gain_term, jnp.stack([query_cot, key_cot])), ('dp', 'mp'))]
    dot_general x14 -> x0, matrix products: 54.8 us -> none  [the longest x4 25.6 us: contract_last(): lax.dot_general(left, right, (((1,), (1,)), ((), ())), preferred_element_...]
    unnamed x48 -> x9, local copies, waits for them, and re-layouts: 14.4 us -> 0.85 us
  transfers between devices with their start and end apart: 4 -> 0, of which waited for: 4 -> 0; matrix products, arithmetic and copies ran while one was open for 6% -> 0% of each run, Pallas kernels for 0% -> 0%
where the time goes in v1:
time: 171 us; the launch traced here: 169 us
  Pallas kernels  157 us (92%)
  other arithmetic  10 us (6%)
    pallas_call x1, Pallas kernels, per_device(): pl.pallas_call(kernel, name='block', out_shape=(jax.ShapeDtypeStruct((ROW...  157 us

profile of v1, /device:TPU:10, one launch (start us, length us, event | category | flops | bytes accessed | tf_op | source)
XLA Modules:
  0.0 169.2 jit_solution(10302574005995903054)
XLA Ops:
  0.6 0.0 copy-start.3
  0.6 156.9 %block.1 = (bf16[16,6144]{1,0:T(8,128)(2,1)}, f32[2,32,128]{2,1,0:T(8,128)}, bf16[3,1536,128]{2,1,0:T(8,128)(2,1)}, bf16[1536,384]{1,0:T(8,128)(2,1)}, bf16[512,1536]{1,0:T(8,128)(2,1)}) custom-call(bf16[16,6144]{1,0:T(8,128)(2,1)} %tok_ref.1, bf16[16,6144]{1,0:T(8,128)(2,1)} %og_ref.1, f32[1,6144]{1,0:T(1,128)} %bitcast.10, f32[1,128]{1,0:T(1,128)} %bitcast.12, ...), custom_call_target="tpu_custom_call" | custom-call | flops 20999999488 | bytes 20000000 | tf_op jit(solution)/shard_map/block/pallas_call | solution.py:502
  157.6 1.3 add_bitcast_fusion
  158.8 0.7 slice.15
  159.6 0.0 copy-done.3
  159.6 0.6 div.3
  160.2 0.0 copy-start.1
  160.2 2.0 %slice_convert_fusion.1 = f32[128,1536]{1,0:T(8,128)} fusion(bf16[512,1536]{1,0:T(8,128)(2,1)} %get-tuple-element.16), kind=kLoop, calls=%fused_computation.2 | loop fusion | flops 196608 | bytes 1179648 | tf_op jit(solution)/shard_map/convert_element_type | solution.py:531
  162.2 3.0 %slice_convert_fusion = f32[384,1536]{1,0:T(8,128)} fusion(bf16[512,1536]{1,0:T(8,128)(2,1)} %get-tuple-element.16), kind=kLoop, calls=%fused_computation.1 | loop fusion | flops 589824 | bytes 3538944 | tf_op jit(solution)/shard_map/convert_element_type | solution.py:532
  165.2 0.0 copy-done.1
  165.2 0.0 copy-start
  165.2 1.6 convert_bitcast_fusion
  166.8 0.2 copy-done
  166.9 0.0 copy-start.2
  166.9 1.6 convert_element_type.17
  168.5 0.0 copy-done.2
  168.5 0.7 copy.17
Async XLA Ops:
  0.6 158.9 %copy-start.3 = (f32[6144]{0:T(1024)S(1)}, f32[6144]{0:T(1024)}, u32[]{:S(2)}) copy-start(f32[6144]{0:T(1024)} %param.10) | copy-start | bytes 73732
  160.2 5.0 %copy-start.1 = (bf16[3,1536,128]{2,1,0:T(8,128)(2,1)S(1)}, bf16[3,1536,128]{2,1,0:T(8,128)(2,1)}, u32[]{:S(2)}) copy-start(bf16[3,1536,128]{2,1,0:T(8,128)(2,1)} %get-tuple-element.14) | copy-start | bytes 3538948
  165.2 1.7 %copy-start = (bf16[1536,384]{1,0:T(8,128)(2,1)S(1)}, bf16[1536,384]{1,0:T(8,128)(2,1)}, u32[]{:S(2)}) copy-start(bf16[1536,384]{1,0:T(8,128)(2,1)} %get-tuple-element.15) | copy-start | bytes 3538948
  166.9 1.6 copy-start.2

commit v2 on v1

--- a/solution.py
+++ b/solution.py
@@ -18,6 +18,7 @@
 W_OUT = HEAD + UP
 ROWS = 16
 TILE = 256
+WIDE = 512
 PART = (slice(0, HALF // 2), slice(HALF // 2, HALF))
 EPS = 1e-06
 GELU_A, GELU_B = 0.7978845608028654, 0.044715
@@ -28,8 +29,8 @@
 
 
 def kernel(
-    tok_ref, og_ref, gain_ref, qg_ref, kg_ref, wqkv_ref, wup_ref, wproj_ref, wdown_ref,
-    tg_ref, gsum_ref, dqkv_ref, dup_ref, dout_ref,
+    tok_ref, og_ref, gain_ref, gain_rows_ref, qg_ref, kg_ref, wqkv_ref, wup_ref, wproj_ref, wdown_ref,
+    tg_ref, gsum_ref, qk_ref, dqkv_ref, dup_ref, dproj_ref, ddown_ref,
     nrm, N, C, G, win, wout, XS, XR, H, HG, ACT, FB1, MB1, FB2, MB2, FS, MS, YR,
     SD, RD, SO, RO, GS, GQ, GC, GY, GX, GZ,
     wsem, y_s, y_r, ag_s, ag_r, e_s, e_r, rs_s, rs_r, z_s, z_r, d_s, d_r, g_s, g_r,
@@ -73,18 +74,16 @@
     for peer in peers:
         pl.semaphore_signal(barrier, inc=1, device_id=peer, device_id_type=MESH)
 
+    zrow = pl.ds(pl.multiple_of(z * ROWS, ROWS), ROWS)
+
     tok = tok_ref[...].astype(F32)
     scale = lax.rsqrt(jnp.mean(tok * tok, axis=1, keepdims=True) + EPS)
     nrm[...] = (tok * scale * gain_ref[...]).astype(BF16)
-    zrow = pl.ds(pl.multiple_of(z * ROWS, ROWS), ROWS)
     N[y_lo, y_hi, x, zrow, :] = nrm[:, half]
     C[y_lo, y_hi, x, zrow, :] = og_ref[:, half]
-    GS[...] = jnp.zeros_like(GS)
-    GQ[...] = jnp.zeros_like(GQ)
     pl.semaphore_wait(barrier, len(peers))
 
-    y_copies = []
-    for a, (src, dst) in enumerate(((nrm, N), (og_ref, C))):
+    def along_y(a, src, dst):
         row = []
         for dy in (1, 2, 3):
             there = ((y + dy) % 4) // 2
@@ -93,7 +92,12 @@
                 send(src.at[:, cols], dst.at[y_lo, y_hi, x, zrow, :],
                      y_s.at[a, dy - 1], y_r.at[a, dy - 1], dev(dy=dy))
             )
-        y_copies.append(row)
+        return row
+
+    y_in = along_y(0, nrm, N)
+    y_out = along_y(1, og_ref, C)
+    GS[...] = jnp.zeros_like(GS)
+    GQ[...] = jnp.zeros_like(GQ)
 
     def zr(i):
         return pl.ds(pl.multiple_of(((z + i) % 4) * ROWS, ROWS), ROWS)
@@ -117,12 +121,15 @@
     def ag_own(u, phase):
         ref, k = units[u]
         where = (ag_first, ag_second)[phase]
-        for p in (0, 1):
-            for d, step in enumerate((1, -1)):
-                block = where(ref, k, p, 0, slice(None))
-                ag[u, phase, 0, p, d] = send(
-                    block, block, ag_s.at[u, phase, p, d], ag_r.at[u, phase, p, d], ag_dev(p, phase, step)
-                )
+        for first in (0, 1):
+            for p in (0, 1):
+                for d, step in enumerate((1, -1)):
+                    yh = d if first == 0 else 1 - d
+                    block = where(ref, k, p, 0, yh)
+                    ag[u, phase, first, p, d] = send(
+                        block, block, ag_s.at[u, phase, p, d, first], ag_r.at[u, phase, p, d, first],
+                        ag_dev(p, phase, step),
+                    )
 
     def ag_fwd(u, phase):
         ref, k = units[u]
@@ -131,15 +138,20 @@
             for d, step in enumerate((1, -1)):
                 ag[u, phase, 0, p, d].wait_recv()
                 block = where(ref, k, p, -step, d)
-                ag[u, phase, 1, p, d] = send(
-                    block, block, ag_s.at[u, phase, p, 2 + d], ag_r.at[u, phase, p, 2 + d],
+                ag[u, phase, 2, p, d] = send(
+                    block, block, ag_s.at[u, phase, p, d, 2], ag_r.at[u, phase, p, d, 2],
                     ag_dev(p, phase, step),
                 )
 
-    def ag_end(u, phase):
+    def ag_wait(u, phase, i):
         for p in (0, 1):
             for d in (0, 1):
-                ag[u, phase, 1, p, d].wait_recv()
+                ag[u, phase, i, p, d].wait_recv()
+
+    def ag_end(u, phase):
+        if phase == 0:
+            ag_wait(u, phase, 1)
+        ag_wait(u, phase, 2)
 
     partner = dev(dy=2)
 
@@ -231,19 +243,19 @@
             slope = 0.5 * (1.0 + t) + 0.5 * u * (1.0 - t * t) * (GELU_A * (1.0 + 3.0 * GELU_B * (u * u)))
             HG[k, y_hi, rows, 3 * HEAD :] = (dact * slope).astype(BF16)
 
-        return (
-            send(HG.at[k, y_hi], HG.at[k, y_hi], e_s.at[k, 2], e_r.at[k, 2], partner),
-            send(ACT.at[k, y_hi], ACT.at[k, y_hi], e_s.at[k, 3], e_r.at[k, 3], partner),
-        )
+        return send(HG.at[k, y_hi], HG.at[k, y_hi], e_s.at[k, 2], e_r.at[k, 2], partner)
+
+    def swap_act(k):
+        return send(ACT.at[k, y_hi], ACT.at[k, y_hi], e_s.at[k, 3], e_r.at[k, 3], partner)
 
     def normed_grad(k, yh):
-        @pl.loop(0, HALF // TILE)
+        @pl.loop(0, HALF // WIDE)
         def _(j):
-            cols = pl.ds(pl.multiple_of(j * TILE, TILE), TILE)
+            cols = pl.ds(pl.multiple_of(j * WIDE, WIDE), WIDE)
             ng = dot(HG[k, yh], win[cols, :], ((1,), (1,)))
-            G[k, yh, :, :, cols] = ng.astype(BF16).reshape(4, 64, TILE)
-            term = ng * N[k, yh, :, :, cols].reshape(PATCHES, TILE).astype(F32)
-            GS[:, cols] += jnp.sum(term.reshape(PATCHES // 8, 8, TILE), axis=0)
+            G[k, yh, :, :, cols] = ng.astype(BF16).reshape(4, 64, WIDE)
+            term = ng * N[k, yh, :, :, cols].reshape(PATCHES, WIDE).astype(F32)
+            GS[:, cols] += jnp.sum(term.reshape(PATCHES // 8, 8, WIDE), axis=0)
 
     def rs_bufs(k, phase, p):
         if phase == 1:
@@ -252,47 +264,45 @@
 
     rs = {}
 
-    def rs_start(k, phase):
+    def rs_start(k, phase, yh, tag):
         where = (ag_first, ag_second)[phase]
+        step = 1 - 2 * yh
         for p in (0, 1):
             fr, mr = rs_bufs(k, phase, p)
-            for d, step in enumerate((1, -1)):
-                to = ag_dev(p, phase, step)
-                sems = lambda i: (rs_s.at[k, phase, p, d, i], rs_r.at[k, phase, p, d, i])
-                rs[k, phase, p, d, 0] = send(where(G, k, p, 2, d), fr.at[d], *sems(0), to)
-                rs[k, phase, p, d, 1] = send(where(G, k, p, step, 1 - d), mr.at[d, 1 - d], *sems(1), to)
-
-    def rs_mid(k, phase):
+            far, near = where(G, k, p, 2, yh), where(G, k, p, -step, yh)
+            sems = [(rs_s.at[k, phase, p, yh, i], rs_r.at[k, phase, p, yh, i]) for i in (0, 1)]
+            rs[k, phase, p, tag, 0] = send(far, fr.at[yh], *sems[0], ag_dev(p, phase, step))
+            rs[k, phase, p, tag, 1] = send(near, mr.at[1, yh], *sems[1], ag_dev(p, phase, -step))
+
+    def rs_mid(k, phase, yh, tag):
         where = (ag_first, ag_second)[phase]
+        step = 1 - 2 * yh
         for p in (0, 1):
             fr, mr = rs_bufs(k, phase, p)
-            for d, step in enumerate((1, -1)):
-                to = ag_dev(p, phase, step)
-                rs[k, phase, p, d, 0].wait_recv()
-                block = where(G, k, p, step, d)
-                block[...] = (block[...].astype(F32) + fr[d].astype(F32)).astype(BF16)
-                rs[k, phase, p, d, 2] = send(
-                    block, mr.at[d, d], rs_s.at[k, phase, p, d, 2], rs_r.at[k, phase, p, d, 2], to
-                )
-
-    def rs_end(k, phase):
+            rs[k, phase, p, tag, 0].wait_recv()
+            block = where(G, k, p, step, yh)
+            block[...] = (block[...].astype(F32) + fr[yh].astype(F32)).astype(BF16)
+            rs[k, phase, p, tag, 2] = send(
+                block, mr.at[0, yh], rs_s.at[k, phase, p, yh, 2], rs_r.at[k, phase, p, yh, 2],
+                ag_dev(p, phase, step),
+            )
+
+    def rs_end(k, phase, yh, tag):
         where = (ag_first, ag_second)[phase]
         for p in (0, 1):
             _, mr = rs_bufs(k, phase, p)
-            for d in (0, 1):
-                rs[k, phase, p, d, 1].wait_recv()
-                rs[k, phase, p, d, 2].wait_recv()
-            for yh in (0, 1):
-                block = where(G, k, p, 0, yh)
-                total = block[...].astype(F32) + mr[0, yh].astype(F32) + mr[1, yh].astype(F32)
-                block[...] = total.astype(BF16)
+            rs[k, phase, p, tag, 1].wait_recv()
+            rs[k, phase, p, tag, 2].wait_recv()
+            block = where(G, k, p, 0, yh)
+            total = block[...].astype(F32) + mr[0, yh].astype(F32) + mr[1, yh].astype(F32)
+            block[...] = total.astype(BF16)
 
     def feature_tile(t, whose):
         return pl.ds(pl.multiple_of(whose * QUART + t * TILE, TILE), TILE)
 
-    def grad_in(t, whose):
-        left = N[:, :, :, :, feature_tile(t, whose)].reshape(4 * PATCHES, TILE)
-        return dot(left, HG[...].reshape(4 * PATCHES, W_IN), ((0,), (0,)))
+    def grad_in(t, whose, k):
+        left = N[k, :, :, :, feature_tile(t, whose)].reshape(2 * PATCHES, TILE)
+        return dot(left, HG[k].reshape(2 * PATCHES, W_IN), ((0,), (0,)))
 
     def grad_out(t, whose):
         right = C[:, :, :, :, feature_tile(t, whose)].reshape(4 * PATCHES, TILE)
@@ -304,35 +314,50 @@
 
     tiles = QUART // TILE
 
-    def grads_away():
+    def tile_rows(t):
+        return pl.ds(pl.multiple_of(t * TILE, TILE), TILE)
+
+    def keep_in(t, total):
+        for j in range(3):
+            dqkv_ref[j, tile_rows(t), :] = total[:, j * HEAD : (j + 1) * HEAD].astype(BF16)
+        dup_ref[tile_rows(t), :] = total[:, 3 * HEAD :].astype(BF16)
+
+    def in_first():
         @pl.loop(0, tiles)
         def _(t):
-            SD[t] = grad_in(t, 1 - core).astype(BF16)
+            SD[t] = grad_in(t, 1 - core, 0).astype(BF16)
+            keep_in(t, grad_in(t, core, 0))
+
+    def in_away(lo, hi):
+        @pl.loop(lo, hi)
+        def _(t):
+            SD[t] = (SD[t].astype(F32) + grad_in(t, 1 - core, 1)).astype(BF16)
             swap(0, t).start()
 
-        @pl.loop(0, tiles)
+    def out_away(lo, hi):
+        @pl.loop(lo, hi)
         def _(t):
             SO[t] = grad_out(t, 1 - core).astype(BF16)
             swap(1, t).start()
 
-    def grads_in_here():
-        @pl.loop(0, tiles)
+    def in_here(lo, hi):
+        @pl.loop(lo, hi)
         def _(t):
-            own = grad_in(t, core)
+            second = grad_in(t, core, 1)
             swap(0, t).wait_recv()
-            rows = pl.ds(pl.multiple_of(t * TILE, TILE), TILE)
-            total = own + RD[t].astype(F32)
-            for j in range(3):
-                dqkv_ref[j, rows, :] = total[:, j * HEAD : (j + 1) * HEAD].astype(BF16)
-            dup_ref[rows, :] = total[:, 3 * HEAD :].astype(BF16)
-
-    def grads_out_here():
-        @pl.loop(0, tiles)
+            kept = [dqkv_ref[j, tile_rows(t), :] for j in range(3)] + [dup_ref[tile_rows(t), :]]
+            first = jnp.concatenate(kept, axis=1).astype(F32)
+            keep_in(t, first + second + RD[t].astype(F32))
+
+    def out_here(lo, hi):
+        @pl.loop(lo, hi)
         def _(t):
             own = grad_out(t, core)
             swap(1, t).wait_recv()
             cols = pl.ds(pl.multiple_of(t * TILE, TILE), TILE)
-            dout_ref[:, cols] = (own + RO[t].astype(F32)).astype(BF16)
+            total = (own + RO[t].astype(F32)).astype(BF16)
+            dproj_ref[:, cols] = total[:HEAD]
+            ddown_ref[:, cols] = total[HEAD:]
 
     def gain_send(stage, slots, me, tos):
         return [
@@ -344,87 +369,128 @@
         for cp in cps:
             cp.wait_recv()
 
-    wait_all(y_copies[0])
+    def owner_copy(dy):
+        yy = (y + dy) % 4
+        return copy(
+            G.at[yy % 2, yy // 2, x, zrow, :], YR.at[y], z_s.at[dy - 1], z_r.at[dy - 1], dev(dy=dy)
+        )
+
+    def to_owner(k):
+        @pl.when(y_lo == k)
+        def _():
+            owner_copy(2).start()
+
+        @pl.when(y_lo != k)
+        def _():
+            owner_copy(1).start()
+            owner_copy(3).start()
+
+    own, other = y_hi, 1 - y_hi
+    wait_all(y_in)
     ag_own(0, 0)
-    wait_all(y_copies[1])
+    wait_all(y_out)
     ag_own(1, 0)
     ag_fwd(0, 0)
     ag_end(0, 0)
     ag_own(0, 1)
     ag_fwd(1, 0)
+    ag_own(2, 0)
+    ag_fwd(0, 1)
     ag_end(1, 0)
-    ag_own(1, 1)
-    ag_own(2, 0)
+    ag_fwd(2, 0)
     for cp in loads:
         cp.wait()
-    ag_fwd(0, 1)
-    ag_fwd(2, 0)
-    ag_end(2, 0)
-    ag_own(2, 1)
+    ag_wait(0, 1, 1)
+    ag_own(1, 1)
     ag_own(3, 0)
     ag_end(0, 1)
     e_in0 = partial_in(0)
     ag_fwd(1, 1)
+    ag_end(2, 0)
     ag_fwd(3, 0)
-    ag_end(3, 0)
-    ag_own(3, 1)
+    ag_wait(1, 1, 1)
+    ag_own(2, 1)
     ag_end(1, 1)
     e_out0 = partial_out(0)
     ag_fwd(2, 1)
+    ag_end(3, 0)
+    ag_wait(2, 1, 1)
+    ag_own(3, 1)
     wait_all((e_in0, e_out0))
     back0 = middle(0)
+    normed_grad(0, own)
     ag_end(2, 1)
     e_in1 = partial_in(1)
     ag_fwd(3, 1)
-    normed_grad(0, y_hi)
-    wait_all(back0)
-    normed_grad(0, 1 - y_hi)
-    rs_start(0, 1)
+    back0.wait_recv()
+    normed_grad(0, other)
+    ag_wait(3, 1, 1)
     ag_end(3, 1)
+    rs_start(0, 1, own, 0)
+    rs_start(0, 1, other, 1)
     e_out1 = partial_out(1)
-    rs_mid(0, 1)
+    in_first()
     wait_all((e_in1, e_out1))
     back1 = middle(1)
-    rs_end(0, 1)
-    rs_start(0, 0)
-    normed_grad(1, y_hi)
-    rs_mid(0, 0)
-    wait_all(back1)
-    normed_grad(1, 1 - y_hi)
-    rs_start(1, 1)
-    rs_end(0, 0)
+    rs_mid(0, 1, own, 0)
+    rs_mid(0, 1, other, 1)
+    normed_grad(1, own)
+    rs_start(1, 1, own, 0)
+    rs_end(0, 1, own, 0)
+    rs_start(0, 0, own, 0)
+    rs_end(0, 1, other, 1)
+    rs_start(0, 0, other, 1)
+    back1.wait_recv()
+    acts = [swap_act(0), swap_act(1)]
+    normed_grad(1, other)
+    rs_start(1, 1, other, 1)
+    rs_mid(0, 0, own, 0)
+    rs_mid(0, 0, other, 1)
+    rs_mid(1, 1, own, 0)
     gsum = jnp.sum(GS[...], axis=0, keepdims=True)
     for j in range(HALF // HEAD):
         GC[core, j : j + 1, :] = gsum[:, j * HEAD : (j + 1) * HEAD]
     GC[core, 24:32, :] = GQ[...]
     g0 = gain_send(0, GC, core, [dev(dc=1)])
-    grads_away()
-    rs_mid(1, 1)
+    in_away(0, 6)
+    rs_end(0, 0, own, 0)
+    rs_end(0, 0, other, 1)
+    to_owner(0)
+    rs_mid(1, 1, other, 1)
     wait_all(g0)
     GY[y] = GC[0] + GC[1]
     g1 = gain_send(1, GY, y, [dev(dy=d) for d in (1, 2, 3)])
-    grads_in_here()
-    rs_end(1, 1)
-    rs_start(1, 0)
+    in_here(0, 6)
+    rs_end(1, 1, own, 0)
+    rs_start(1, 0, own, 0)
+    wait_all(acts)
+    out_away(0, 3)
+    rs_end(1, 1, other, 1)
+    rs_start(1, 0, other, 1)
+    out_away(3, 6)
+    rs_mid(1, 0, own, 0)
     wait_all(g1)
     GX[x, 0] = GY[0] + GY[1]
     GX[x, 1] = GY[2] + GY[3]
     g2 = gain_send(2, GX, x, [dev(dx=d) for d in (1, 2, 3)])
-    rs_mid(1, 0)
-    grads_out_here()
-    rs_end(1, 0)
-
-    last = []
-    for dy in (1, 2, 3):
-        yy = (y + dy) % 4
-        last.append(
-            send(G.at[yy % 2, yy // 2, x, zrow, :], YR.at[y], z_s.at[dy - 1], z_r.at[dy - 1], dev(dy=dy))
-        )
+    rs_mid(1, 0, other, 1)
+    out_here(0, 2)
+    rs_end(1, 0, own, 0)
+    rs_end(1, 0, other, 1)
+    to_owner(1)
     YR[y] = G[y_lo, y_hi, x, zrow, :]
     wait_all(g2)
     GZ[z] = ((GX[0] + GX[1]) + GX[2]) + GX[3]
     g3 = gain_send(3, GZ, z, [dev(dz=d) for d in (1, 2, 3)])
-    wait_all(last)
+    out_here(2, 6)
+    wait_all(g3)
+    gains = ((GZ[0] + GZ[1]) + GZ[2]) + GZ[3]
+    for h in (0, 1):
+        rows = slice(h * 24, (h + 1) * 24)
+        gsum_ref[rows, :] = gains[h, 0:24, :] / gain_rows_ref[rows, :]
+    qk_ref[...] = gains[0, 24:26, :] + gains[1, 24:26, :]
+    for dy in (1, 2, 3):
+        owner_copy(dy).wait_recv()
     inner = jnp.zeros((ROWS, 1), F32)
     for h in (0, 1):
         cols = slice(h * HALF, (h + 1) * HALF)
@@ -437,11 +503,10 @@
         own = tok_ref[:, cols].astype(F32)
         grad = og_ref[:, cols].astype(F32) + scale * c - own * (scale * scale * scale * inner)
         tg_ref[:, cols] = grad.astype(BF16)
-    wait_all(g3)
-    gsum_ref[...] = ((GZ[0] + GZ[1]) + GZ[2]) + GZ[3]
-
     for cp in pending:
         cp.wait_send()
+    for dy in (1, 2, 3):
+        owner_copy(dy).wait_send()
 
     @pl.loop(0, tiles)
     def _(t):
@@ -486,8 +551,8 @@
         dma((6,)),
         dma((2, 3)),
         dma((2, 3)),
-        dma((4, 2, 2, 4)),
-        dma((4, 2, 2, 4)),
+        dma((4, 2, 2, 2, 3)),
+        dma((4, 2, 2, 2, 3)),
         dma((2, 4)),
         dma((2, 4)),
         dma((2, 2, 2, 2, 3)),
@@ -499,38 +564,62 @@
         dma((4, 3)),
         dma((4, 3)),
     ]
-    token_grad, gains, dqkv, dup, dout = pl.pallas_call(
+    token_grad, gain_grad, qk_grad, dqkv, dup, dproj, ddown = pl.pallas_call(
         kernel,
         name="block",
         out_shape=(
             jax.ShapeDtypeStruct((ROWS, D), BF16),
-            jax.ShapeDtypeStruct((2, 32, HEAD), F32),
+            jax.ShapeDtypeStruct((D // HEAD, HEAD), F32),
+            jax.ShapeDtypeStruct((2, HEAD), F32),
             jax.ShapeDtypeStruct((3, QUART, HEAD), BF16),
             jax.ShapeDtypeStruct((QUART, UP), BF16),
-            jax.ShapeDtypeStruct((W_OUT, QUART), BF16),
+            jax.ShapeDtypeStruct((HEAD, QUART), BF16),
+            jax.ShapeDtypeStruct((UP, QUART), BF16),
         ),
-        in_specs=[vm] * 5 + [hbm] * 4,
-        out_specs=(vm,) * 5,
+        in_specs=[vm] * 6 + [hbm] * 4,
+        out_specs=(vm,) * 7,
         scratch_shapes=scratch,
         compiler_params=pltpu.CompilerParams(
             collective_id=0, has_side_effects=True, vmem_limit_bytes=60 * 1024 * 1024
         ),
         cost_estimate=pl.CostEstimate(flops=21 * 10**9, bytes_accessed=20 * 10**6, transcendentals=0),
     )(
-        tokens, out_grad, norm_gain.reshape(1, D), query_gain.reshape(1, HEAD), key_gain.reshape(1, HEAD),
+        tokens, out_grad, norm_gain.reshape(1, D), norm_gain.reshape(D // HEAD, HEAD),
+        query_gain.reshape(1, HEAD), key_gain.reshape(1, HEAD),
         jnp.transpose(qkv_weight, (1, 0, 2)), up_weight, proj_weight, down_weight,
     )
-    norm_gain_grad = gains[:, : HALF // HEAD].reshape(D) / norm_gain
-    qk_gain_grad = gains[0, 24:26] + gains[1, 24:26]
-    return (
-        token_grad,
-        norm_gain_grad,
-        qk_gain_grad,
-        jnp.transpose(dqkv, (1, 0, 2)).astype(F32),
-        dup.astype(F32),
-        dout[:HEAD].astype(F32),
-        dout[HEAD:].astype(F32),
-    )
+    return finish(token_grad, gain_grad, qk_grad, dqkv, dup, dproj, ddown)
+
+
+def widen(tg_ref, gain_ref, qk_ref, dqkv_ref, dup_ref, dproj_ref, ddown_ref, *outs):
+    tg_out, gain_out, qk_out, dqkv_out, dup_out, dproj_out, ddown_out = outs
+
+    @pl.when(pl.program_id(0) == 0)
+    def _():
+        tg_out[...] = tg_ref[...]
+        gain_out[...] = gain_ref[...]
+        qk_out[...] = qk_ref[...]
+
+    for src, dst in ((dqkv_ref, dqkv_out), (dup_ref, dup_out), (dproj_ref, dproj_out), (ddown_ref, ddown_out)):
+        dst[...] = src[...].astype(F32)
+
+
+def finish(*arrays):
+    steps = 6
+    block = QUART // steps
+    whole = [pl.BlockSpec(a.shape, lambda i: (0, 0)) for a in arrays[:3]]
+    specs = whole + [
+        pl.BlockSpec((3, block, HEAD), lambda i: (0, i, 0)),
+        pl.BlockSpec((block, UP), lambda i: (i, 0)),
+        pl.BlockSpec((HEAD, block), lambda i: (0, i)),
+        pl.BlockSpec((UP, block), lambda i: (0, i)),
+    ]
+    shapes = [jax.ShapeDtypeStruct(a.shape, a.dtype) for a in arrays[:3]]
+    shapes += [jax.ShapeDtypeStruct(a.shape, F32) for a in arrays[3:]]
+    token_grad, gain_grad, qk_grad, dqkv, dup, dproj, ddown = pl.pallas_call(
+        widen, name="widen", grid=(steps,), in_specs=specs, out_specs=specs, out_shape=shapes
+    )(*arrays)
+    return token_grad, gain_grad.reshape(D), qk_grad, jnp.transpose(dqkv, (1, 0, 2)), dup, dproj, ddown
 
 
 def solution(mesh):

time: 171 us -> 144 us (0.84); the launches traced: 169 us -> 144 us
  Pallas kernels: 157 us -> 143 us
  other arithmetic: 10 us -> 0 us
    pallas_call x1, Pallas kernels: 157 us -> 137 us  [per_device(): pl.pallas_call(kernel, name='block', out_shape=(jax.ShapeDtypeStruct((ROW...]
    convert_element_type x4 -> x0, other arithmetic: 8.13 us -> none  [the longest x1 2.97 us: per_device(): dout[HEAD:].astype(F32)]
    pallas_call x0 -> x1, Pallas kernels: none -> 6.81 us  [finish(): pl.pallas_call(widen, name='widen', grid=(steps,), in_specs=specs, out_sp...]
where the time goes in v2:
time: 144 us
  Pallas kernels  143 us (99%)
    pallas_call x1, Pallas kernels, per_device(): pl.pallas_call(kernel, name='block', out_shape=(jax.ShapeDtypeStruct((ROW...  137 us
    pallas_call x1, Pallas kernels, finish(): pl.pallas_call(widen, name='widen', grid=(steps,), in_specs=specs, out_sp...  6.81 us

profile of v2, /device:TPU:10, one launch (start us, length us, event | category | flops | bytes accessed | tf_op | source)
XLA Modules:
  0.0 144.1 jit_solution(10086102559765541669)
XLA Ops:
  0.6 136.6 %block.1 = (bf16[16,6144]{1,0:T(8,128)(2,1)}, f32[48,128]{1,0:T(8,128)}, f32[2,128]{1,0:T(2,128)}, bf16[3,1536,128]{2,1,0:T(8,128)(2,1)}, bf16[1536,384]{1,0:T(8...) custom-call(bf16[16,6144]{1,0:T(8,128)(2,1)} %tok_ref.1, bf16[16,6144]{1,0:T(8,128)(2,1)} %og_ref.1, ...), custom_call_target="tpu_custom_call" | custom-call | flops 20999999488 | bytes 20000000 | tf_op jit(solution)/shard_map/block/pallas_call | solution.py:567
  137.3 6.8 %widen.1 = (bf16[16,6144]{1,0:T(8,128)(2,1)}, f32[48,128]{1,0:T(8,128)}, f32[2,128]{1,0:T(2,128)}, f32[3,1536,128]{2,1,0:T(8,128)}, f32[1536,384]{1,0:T(8,128)},...) custom-call(bf16[16,6144]{1,0:T(8,128)(2,1)} %get-tuple-element.21.tg_ref, f32[48,128]{1,0:T(8,128)} %get-tuple-element.22.gain_ref, ...), custom_call_target="tpu_custom_call" | custom-call | tf_op jit(solution)/shard_map/widen/pallas_call | solution.py:619

commit v3 on v2

--- a/solution.py
+++ b/solution.py
@@ -20,6 +20,7 @@
 TILE = 256
 WIDE = 512
 PART = (slice(0, HALF // 2), slice(HALF // 2, HALF))
+SUB = HALF // 4
 EPS = 1e-06
 GELU_A, GELU_B = 0.7978845608028654, 0.044715
 
@@ -30,10 +31,10 @@
 
 def kernel(
     tok_ref, og_ref, gain_ref, gain_rows_ref, qg_ref, kg_ref, wqkv_ref, wup_ref, wproj_ref, wdown_ref,
-    tg_ref, gsum_ref, qk_ref, dqkv_ref, dup_ref, dproj_ref, ddown_ref,
+    tg_ref, gsum_ref, qk_ref, dqkv_hbm, dup_hbm, dproj_hbm, ddown_hbm,
     nrm, N, C, G, win, wout, XS, XR, H, HG, ACT, FB1, MB1, FB2, MB2, FS, MS, YR,
     SD, RD, SO, RO, GS, GQ, GC, GY, GX, GZ,
-    wsem, y_s, y_r, ag_s, ag_r, e_s, e_r, rs_s, rs_r, z_s, z_r, d_s, d_r, g_s, g_r,
+    dqkv_ref, dup_ref, dproj_ref, ddown_ref, osem, wsem, y_s, y_r, ag_s, ag_f, ag_r, e_s, e_r, rs_s, rs_f, rs_r, z_s, z_r, d_s, d_r, g_s, g_r,
 ):
     dp, mp = lax.axis_index("dp"), lax.axis_index("mp")
     y_hi, core = dp // 2, dp % 2
@@ -50,6 +51,26 @@
         )
 
     pending = []
+
+    def begin(*args):
+        cp = copy(*args)
+        cp.start()
+        return cp
+
+    def take(sem, view):
+        pltpu.make_async_copy(view, view, sem).wait()
+
+    def blocks(count):
+        rows, cols = {2: (32, 1), 6: (32, 1), 24: (64, 2)}.get(count, (64, 1))
+        groups = count * ROWS // (rows * cols)
+        if count == 48:
+            return N.at[0, :, 0:3]
+        return N.at[0, 0, 0:groups, 0:rows, 0 : cols * (HALF // 2)]
+
+    def drain(upto):
+        for cp in pending[:upto]:
+            cp.wait_send()
+        del pending[:upto]
 
     def send(*args):
         cp = copy(*args)
@@ -84,18 +105,33 @@
     pl.semaphore_wait(barrier, len(peers))
 
     def along_y(a, src, dst):
-        row = []
+        row = {}
         for dy in (1, 2, 3):
             there = ((y + dy) % 4) // 2
             cols = pl.ds(pl.multiple_of(there * HALF, HALF), HALF)
-            row.append(
-                send(src.at[:, cols], dst.at[y_lo, y_hi, x, zrow, :],
-                     y_s.at[a, dy - 1], y_r.at[a, dy - 1], dev(dy=dy))
-            )
+            row[dy] = copy(src.at[:, cols], dst.at[y_lo, y_hi, x, zrow, :],
+                           y_s.at[a, dy - 1], y_r.at[a, dy - 1], dev(dy=dy))
         return row
 
-    y_in = along_y(0, nrm, N)
-    y_out = along_y(1, og_ref, C)
+    y_copies = [along_y(0, nrm, N), along_y(1, og_ref, C)]
+
+    def y_start(a, k):
+        @pl.when(y_lo == k)
+        def _():
+            for dy in (1, 3, 2):
+                y_copies[a][dy].start()
+
+    def y_wait(a, k):
+        @pl.when(y_lo == k)
+        def _():
+            y_copies[a][2].wait_recv()
+
+        @pl.when(y_lo != k)
+        def _():
+            y_copies[a][1].wait_recv()
+            y_copies[a][3].wait_recv()
+
+    y_start(0, 0)
     GS[...] = jnp.zeros_like(GS)
     GQ[...] = jnp.zeros_like(GQ)
 
@@ -124,34 +160,33 @@
         for first in (0, 1):
             for p in (0, 1):
                 for d, step in enumerate((1, -1)):
-                    yh = d if first == 0 else 1 - d
-                    block = where(ref, k, p, 0, yh)
-                    ag[u, phase, first, p, d] = send(
-                        block, block, ag_s.at[u, phase, p, d, first], ag_r.at[u, phase, p, d, first],
-                        ag_dev(p, phase, step),
-                    )
+                    block = where(ref, k, p, 0, d if first == 0 else 1 - d)
+                    recv = ag_f.at[u, phase, p, d] if first == 0 else ag_r.at[u, phase, 0]
+                    cp = begin(block, block, ag_s.at[u, phase], recv, ag_dev(p, phase, step))
+                    if first == 0:
+                        ag[u, phase, p, d] = cp
 
     def ag_fwd(u, phase):
         ref, k = units[u]
         where = (ag_first, ag_second)[phase]
         for p in (0, 1):
             for d, step in enumerate((1, -1)):
-                ag[u, phase, 0, p, d].wait_recv()
+                ag[u, phase, p, d].wait_recv()
                 block = where(ref, k, p, -step, d)
-                ag[u, phase, 2, p, d] = send(
-                    block, block, ag_s.at[u, phase, p, d, 2], ag_r.at[u, phase, p, d, 2],
-                    ag_dev(p, phase, step),
-                )
+                begin(block, block, ag_s.at[u, phase], ag_r.at[u, phase, 1], ag_dev(p, phase, step))
 
     def ag_wait(u, phase, i):
-        for p in (0, 1):
-            for d in (0, 1):
-                ag[u, phase, i, p, d].wait_recv()
+        take(ag_r.at[u, phase, i - 1], blocks((4, 16)[phase]))
 
     def ag_end(u, phase):
         if phase == 0:
             ag_wait(u, phase, 1)
         ag_wait(u, phase, 2)
+
+    def ag_sent():
+        for u in range(4):
+            for phase in (0, 1):
+                take(ag_s.at[u, phase], blocks((12, 48)[phase]))
 
     partner = dev(dy=2)
 
@@ -262,41 +297,54 @@
             return (FB1, FB2)[p].at[k], (MB1, MB2)[p].at[k]
         return FS.at[p, k], MS.at[p, k]
 
-    rs = {}
-
-    def rs_start(k, phase, yh, tag):
+    def rs_cut(phase, p, view, s):
+        cols = pl.ds(s * SUB, SUB)
+        return view.at[:, :, cols] if phase == 1 and p == 0 else view.at[:, cols]
+
+    def rs_steps(k, phase, yh):
         where = (ag_first, ag_second)[phase]
-        step = 1 - 2 * yh
         for p in (0, 1):
             fr, mr = rs_bufs(k, phase, p)
-            far, near = where(G, k, p, 2, yh), where(G, k, p, -step, yh)
-            sems = [(rs_s.at[k, phase, p, yh, i], rs_r.at[k, phase, p, yh, i]) for i in (0, 1)]
-            rs[k, phase, p, tag, 0] = send(far, fr.at[yh], *sems[0], ag_dev(p, phase, step))
-            rs[k, phase, p, tag, 1] = send(near, mr.at[1, yh], *sems[1], ag_dev(p, phase, -step))
-
-    def rs_mid(k, phase, yh, tag):
-        where = (ag_first, ag_second)[phase]
-        step = 1 - 2 * yh
-        for p in (0, 1):
-            fr, mr = rs_bufs(k, phase, p)
-            rs[k, phase, p, tag, 0].wait_recv()
-            block = where(G, k, p, step, yh)
-            block[...] = (block[...].astype(F32) + fr[yh].astype(F32)).astype(BF16)
-            rs[k, phase, p, tag, 2] = send(
-                block, mr.at[0, yh], rs_s.at[k, phase, p, yh, 2], rs_r.at[k, phase, p, yh, 2],
-                ag_dev(p, phase, step),
-            )
-
-    def rs_end(k, phase, yh, tag):
+            for s, step in enumerate((1, -1)):
+                block = lambda off: rs_cut(phase, p, where(G, k, p, off, yh), s)
+                far = rs_cut(phase, p, fr.at[yh], s)
+                near = [rs_cut(phase, p, mr.at[i, yh], s) for i in (0, 1)]
+                yield p, step, block, far, near
+
+    def rs_far(k, phase, yh):
+        for p, step, block, far, _ in rs_steps(k, phase, yh):
+            begin(block(2), far, rs_s.at[k, phase, yh], rs_f.at[k, phase, yh], ag_dev(p, phase, step))
+
+    def rs_near(k, phase, yh):
+        for p, step, block, _, near in rs_steps(k, phase, yh):
+            begin(block(-step), near[1], rs_s.at[k, phase, yh], rs_r.at[k, phase, yh], ag_dev(p, phase, -step))
+
+    def rs_start(k, phase, yh):
+        rs_far(k, phase, yh)
+        rs_near(k, phase, yh)
+
+    def rs_mid(k, phase, yh):
+        take(rs_f.at[k, phase, yh], blocks((2, 8)[phase]))
+        for p, step, block, far, near in rs_steps(k, phase, yh):
+            mine = block(step)
+            mine[...] = (mine[...].astype(F32) + far[...].astype(F32)).astype(BF16)
+            begin(mine, near[0], rs_s.at[k, phase, yh], rs_r.at[k, phase, yh], ag_dev(p, phase, step))
+
+    def rs_end(k, phase, yh):
+        take(rs_r.at[k, phase, yh], blocks((4, 16)[phase]))
         where = (ag_first, ag_second)[phase]
         for p in (0, 1):
             _, mr = rs_bufs(k, phase, p)
-            rs[k, phase, p, tag, 1].wait_recv()
-            rs[k, phase, p, tag, 2].wait_recv()
             block = where(G, k, p, 0, yh)
             total = block[...].astype(F32) + mr[0, yh].astype(F32) + mr[1, yh].astype(F32)
             block[...] = total.astype(BF16)
 
+    def rs_sent():
+        for k in (0, 1):
+            for phase in (0, 1):
+                for yh in (0, 1):
+                    take(rs_s.at[k, phase, yh], blocks((6, 24)[phase]))
+
     def feature_tile(t, whose):
         return pl.ds(pl.multiple_of(whose * QUART + t * TILE, TILE), TILE)
 
@@ -304,13 +352,13 @@
         left = N[k, :, :, :, feature_tile(t, whose)].reshape(2 * PATCHES, TILE)
         return dot(left, HG[k].reshape(2 * PATCHES, W_IN), ((0,), (0,)))
 
-    def grad_out(t, whose):
-        right = C[:, :, :, :, feature_tile(t, whose)].reshape(4 * PATCHES, TILE)
-        return dot(ACT[...].reshape(4 * PATCHES, W_OUT), right, ((0,), (0,)))
+    def grad_out(t, whose, yh):
+        right = C[:, yh, :, :, feature_tile(t, whose)].reshape(2 * PATCHES, TILE)
+        return dot(ACT[:, yh].reshape(2 * PATCHES, W_OUT), right, ((0,), (0,)))
 
     def swap(kind, t):
         src, dst = ((SD, RD), (SO, RO))[kind]
-        return copy(src.at[t], dst.at[t], d_s.at[kind, t], d_r.at[kind, t], dev(dc=1))
+        return copy(src.at[t], dst.at[t], d_s.at[kind], d_r.at[kind, t], dev(dc=1))
 
     tiles = QUART // TILE
 
@@ -322,11 +370,21 @@
             dqkv_ref[j, tile_rows(t), :] = total[:, j * HEAD : (j + 1) * HEAD].astype(BF16)
         dup_ref[tile_rows(t), :] = total[:, 3 * HEAD :].astype(BF16)
 
-    def in_first():
-        @pl.loop(0, tiles)
+    def in_first(lo, hi):
+        @pl.loop(lo, hi)
         def _(t):
             SD[t] = grad_in(t, 1 - core, 0).astype(BF16)
             keep_in(t, grad_in(t, core, 0))
+
+    def keep_out(t, total):
+        dproj_ref[:, tile_rows(t)] = total[:HEAD].astype(BF16)
+        ddown_ref[:, tile_rows(t)] = total[HEAD:].astype(BF16)
+
+    def out_first():
+        @pl.loop(0, tiles)
+        def _(t):
+            SO[t] = grad_out(t, 1 - core, y_hi).astype(BF16)
+            keep_out(t, grad_out(t, core, y_hi))
 
     def in_away(lo, hi):
         @pl.loop(lo, hi)
@@ -337,7 +395,7 @@
     def out_away(lo, hi):
         @pl.loop(lo, hi)
         def _(t):
-            SO[t] = grad_out(t, 1 - core).astype(BF16)
+            SO[t] = (SO[t].astype(F32) + grad_out(t, 1 - core, 1 - y_hi)).astype(BF16)
             swap(1, t).start()
 
     def in_here(lo, hi):
@@ -352,18 +410,24 @@
     def out_here(lo, hi):
         @pl.loop(lo, hi)
         def _(t):
-            own = grad_out(t, core)
+            second = grad_out(t, core, 1 - y_hi)
             swap(1, t).wait_recv()
-            cols = pl.ds(pl.multiple_of(t * TILE, TILE), TILE)
-            total = (own + RO[t].astype(F32)).astype(BF16)
-            dproj_ref[:, cols] = total[:HEAD]
-            ddown_ref[:, cols] = total[HEAD:]
+            kept = [dproj_ref[:, tile_rows(t)], ddown_ref[:, tile_rows(t)]]
+            first = jnp.concatenate(kept, axis=0).astype(F32)
+            keep_out(t, first + second + RO[t].astype(F32))
 
     def gain_send(stage, slots, me, tos):
-        return [
-            send(slots.at[me], slots.at[me], g_s.at[stage, i], g_r.at[stage, i], to)
-            for i, to in enumerate(tos)
-        ]
+        for to in tos:
+            begin(slots.at[me], slots.at[me], g_s.at[stage], g_r.at[stage], to)
+
+    gain_slots = [GC.at[0:1], GY.at[0:3], GX.at[0:3], GZ.at[0:3]]
+
+    def gain_wait(stage):
+        take(g_r.at[stage], gain_slots[stage])
+
+    def gain_sent():
+        for stage in range(4):
+            take(g_s.at[stage], gain_slots[stage])
 
     def wait_all(cps):
         for cp in cps:
@@ -385,15 +449,22 @@
             owner_copy(1).start()
             owner_copy(3).start()
 
+    results = ((dqkv_ref, dqkv_hbm), (dup_ref, dup_hbm), (dproj_ref, dproj_hbm), (ddown_ref, ddown_hbm))
+    stores = [pltpu.make_async_copy(src, dst, osem.at[i]) for i, (src, dst) in enumerate(results)]
+
     own, other = y_hi, 1 - y_hi
-    wait_all(y_in)
+    y_wait(0, 0)
+    y_start(1, 0)
     ag_own(0, 0)
-    wait_all(y_out)
+    y_wait(1, 0)
     ag_own(1, 0)
+    y_start(0, 1)
+    y_start(1, 1)
     ag_fwd(0, 0)
     ag_end(0, 0)
     ag_own(0, 1)
     ag_fwd(1, 0)
+    y_wait(0, 1)
     ag_own(2, 0)
     ag_fwd(0, 1)
     ag_end(1, 0)
@@ -402,6 +473,7 @@
         cp.wait()
     ag_wait(0, 1, 1)
     ag_own(1, 1)
+    y_wait(1, 1)
     ag_own(3, 0)
     ag_end(0, 1)
     e_in0 = partial_in(0)
@@ -425,65 +497,74 @@
     back0.wait_recv()
     normed_grad(0, other)
     ag_wait(3, 1, 1)
+    in_first(0, 3)
     ag_end(3, 1)
-    rs_start(0, 1, own, 0)
-    rs_start(0, 1, other, 1)
+    rs_far(0, 1, own)
+    rs_far(0, 1, other)
     e_out1 = partial_out(1)
-    in_first()
+    rs_near(0, 1, own)
+    rs_near(0, 1, other)
+    in_first(3, 6)
+    rs_mid(0, 1, own)
     wait_all((e_in1, e_out1))
     back1 = middle(1)
-    rs_mid(0, 1, own, 0)
-    rs_mid(0, 1, other, 1)
+    rs_mid(0, 1, other)
     normed_grad(1, own)
-    rs_start(1, 1, own, 0)
-    rs_end(0, 1, own, 0)
-    rs_start(0, 0, own, 0)
-    rs_end(0, 1, other, 1)
-    rs_start(0, 0, other, 1)
+    rs_start(1, 1, own)
+    rs_end(0, 1, own)
+    rs_start(0, 0, own)
+    rs_end(0, 1, other)
+    rs_start(0, 0, other)
+    out_first()
     back1.wait_recv()
+    normed_grad(1, other)
+    rs_start(1, 1, other)
     acts = [swap_act(0), swap_act(1)]
-    normed_grad(1, other)
-    rs_start(1, 1, other, 1)
-    rs_mid(0, 0, own, 0)
-    rs_mid(0, 0, other, 1)
-    rs_mid(1, 1, own, 0)
+    rs_mid(0, 0, own)
+    rs_mid(0, 0, other)
+    rs_mid(1, 1, own)
     gsum = jnp.sum(GS[...], axis=0, keepdims=True)
     for j in range(HALF // HEAD):
         GC[core, j : j + 1, :] = gsum[:, j * HEAD : (j + 1) * HEAD]
     GC[core, 24:32, :] = GQ[...]
-    g0 = gain_send(0, GC, core, [dev(dc=1)])
+    gain_send(0, GC, core, [dev(dc=1)])
     in_away(0, 6)
-    rs_end(0, 0, own, 0)
-    rs_end(0, 0, other, 1)
+    rs_mid(1, 1, other)
+    rs_end(0, 0, own)
+    rs_end(0, 0, other)
     to_owner(0)
-    rs_mid(1, 1, other, 1)
-    wait_all(g0)
+    gain_wait(0)
     GY[y] = GC[0] + GC[1]
-    g1 = gain_send(1, GY, y, [dev(dy=d) for d in (1, 2, 3)])
-    in_here(0, 6)
-    rs_end(1, 1, own, 0)
-    rs_start(1, 0, own, 0)
-    wait_all(acts)
-    out_away(0, 3)
-    rs_end(1, 1, other, 1)
-    rs_start(1, 0, other, 1)
-    out_away(3, 6)
-    rs_mid(1, 0, own, 0)
-    wait_all(g1)
+    gain_send(1, GY, y, [dev(dy=d) for d in (1, 2, 3)])
+    rs_end(1, 1, own)
+    rs_start(1, 0, own)
+    in_here(0, 4)
+    rs_end(1, 1, other)
+    rs_start(1, 0, other)
+    in_here(4, 6)
+    for cp in stores[:2]:
+        cp.start()
+    rs_mid(1, 0, own)
+    rs_mid(1, 0, other)
+    gain_wait(1)
     GX[x, 0] = GY[0] + GY[1]
     GX[x, 1] = GY[2] + GY[3]
-    g2 = gain_send(2, GX, x, [dev(dx=d) for d in (1, 2, 3)])
-    rs_mid(1, 0, other, 1)
-    out_here(0, 2)
-    rs_end(1, 0, own, 0)
-    rs_end(1, 0, other, 1)
+    gain_send(2, GX, x, [dev(dx=d) for d in (1, 2, 3)])
+    wait_all(acts)
+    out_away(0, 6)
+    rs_end(1, 0, own)
+    rs_end(1, 0, other)
     to_owner(1)
     YR[y] = G[y_lo, y_hi, x, zrow, :]
-    wait_all(g2)
+    gain_wait(2)
     GZ[z] = ((GX[0] + GX[1]) + GX[2]) + GX[3]
-    g3 = gain_send(3, GZ, z, [dev(dz=d) for d in (1, 2, 3)])
-    out_here(2, 6)
-    wait_all(g3)
+    gain_send(3, GZ, z, [dev(dz=d) for d in (1, 2, 3)])
+    out_here(0, 6)
+    for cp in stores[2:]:
+        cp.start()
+    ag_sent()
+    rs_sent()
+    gain_wait(3)
     gains = ((GZ[0] + GZ[1]) + GZ[2]) + GZ[3]
     for h in (0, 1):
         rows = slice(h * 24, (h + 1) * 24)
@@ -503,15 +584,17 @@
         own = tok_ref[:, cols].astype(F32)
         grad = og_ref[:, cols].astype(F32) + scale * c - own * (scale * scale * scale * inner)
         tg_ref[:, cols] = grad.astype(BF16)
-    for cp in pending:
-        cp.wait_send()
+    gain_sent()
+    drain(len(pending))
+    for cp in stores:
+        cp.wait()
+    for row in y_copies:
+        for dy in (1, 2, 3):
+            row[dy].wait_send()
     for dy in (1, 2, 3):
         owner_copy(dy).wait_send()
-
-    @pl.loop(0, tiles)
-    def _(t):
-        swap(0, t).wait_send()
-        swap(1, t).wait_send()
+    take(d_s.at[0], SD)
+    take(d_s.at[1], SO)
 
 
 def per_device(tokens, norm_gain, qkv_weight, up_weight, proj_weight, down_weight, query_gain, key_gain, out_grad):
@@ -548,21 +631,28 @@
         pltpu.VMEM((4, 32, HEAD), F32),
         pltpu.VMEM((4, 2, 32, HEAD), F32),
         pltpu.VMEM((4, 2, 32, HEAD), F32),
+        pltpu.VMEM((3, QUART, HEAD), BF16),
+        pltpu.VMEM((QUART, UP), BF16),
+        pltpu.VMEM((HEAD, QUART), BF16),
+        pltpu.VMEM((UP, QUART), BF16),
+        dma((4,)),
         dma((6,)),
         dma((2, 3)),
         dma((2, 3)),
-        dma((4, 2, 2, 2, 3)),
-        dma((4, 2, 2, 2, 3)),
+        dma((4, 2)),
+        dma((4, 2, 2, 2)),
+        dma((4, 2, 2)),
         dma((2, 4)),
         dma((2, 4)),
-        dma((2, 2, 2, 2, 3)),
-        dma((2, 2, 2, 2, 3)),
+        dma((2, 2, 2)),
+        dma((2, 2, 2)),
+        dma((2, 2, 2)),
         dma((3,)),
         dma((3,)),
+        dma((2,)),
         dma((2, tiles)),
-        dma((2, tiles)),
-        dma((4, 3)),
-        dma((4, 3)),
+        dma((4,)),
+        dma((4,)),
     ]
     token_grad, gain_grad, qk_grad, dqkv, dup, dproj, ddown = pl.pallas_call(
         kernel,
@@ -577,7 +667,7 @@
             jax.ShapeDtypeStruct((UP, QUART), BF16),
         ),
         in_specs=[vm] * 6 + [hbm] * 4,
-        out_specs=(vm,) * 7,
+        out_specs=(vm,) * 3 + (hbm,) * 4,
         scratch_shapes=scratch,
         compiler_params=pltpu.CompilerParams(
             collective_id=0, has_side_effects=True, vmem_limit_bytes=60 * 1024 * 1024
@@ -605,7 +695,7 @@
 
 
 def finish(*arrays):
-    steps = 6
+    steps = 2
     block = QUART // steps
     whole = [pl.BlockSpec(a.shape, lambda i: (0, 0)) for a in arrays[:3]]
     specs = whole + [

time: 144 us -> 138 us (0.958); the launches traced: 144 us -> 136 us
  Pallas kernels: 143 us -> 135 us
    pallas_call x1, Pallas kernels: 137 us -> 130 us  [per_device(): pl.pallas_call(kernel, name='block', out_shape=(jax.ShapeDtypeStruct((ROW...]
    pallas_call x1, Pallas kernels: 6.81 us -> 5.11 us  [finish(): pl.pallas_call(widen, name='widen', grid=(steps,), in_specs=specs, out_sp...]
where the time goes in v3:
time: 138 us; the launch traced here: 136 us
  Pallas kernels  135 us (98%)
    pallas_call x1, Pallas kernels, per_device(): pl.pallas_call(kernel, name='block', out_shape=(jax.ShapeDtypeStruct((ROW...  130 us
    pallas_call x1, Pallas kernels, finish(): pl.pallas_call(widen, name='widen', grid=(steps,), in_specs=specs, out_sp...  5.11 us

profile of v3, /device:TPU:10, one launch (start us, length us, event | category | flops | bytes accessed | tf_op | source)
XLA Modules:
  0.0 135.8 jit_solution(5638175891375391340)
XLA Ops:
  0.6 130.1 %block.1 = (bf16[16,6144]{1,0:T(8,128)(2,1)}, f32[48,128]{1,0:T(8,128)}, f32[2,128]{1,0:T(2,128)}, bf16[3,1536,128]{2,1,0:T(8,128)(2,1)}, bf16[1536,384]{1,0:T(8...) custom-call(bf16[16,6144]{1,0:T(8,128)(2,1)} %tok_ref.1, bf16[16,6144]{1,0:T(8,128)(2,1)} %og_ref.1, ...), custom_call_target="tpu_custom_call" | custom-call | flops 20999999488 | bytes 20000000 | tf_op jit(solution)/shard_map/block/pallas_call | solution.py:657
  130.7 5.1 %widen.1 = (bf16[16,6144]{1,0:T(8,128)(2,1)}, f32[48,128]{1,0:T(8,128)}, f32[2,128]{1,0:T(2,128)}, f32[3,1536,128]{2,1,0:T(8,128)}, f32[1536,384]{1,0:T(8,128)},...) custom-call(bf16[16,6144]{1,0:T(8,128)(2,1)} %get-tuple-element.21.tg_ref, f32[48,128]{1,0:T(8,128)} %get-tuple-element.22.gain_ref, ...), custom_call_target="tpu_custom_call" | custom-call | tf_op jit(solution)/shard_map/widen/pallas_call | solution.py:709

commit v4 on v3

--- a/solution.py
+++ b/solution.py
@@ -61,7 +61,7 @@
         pltpu.make_async_copy(view, view, sem).wait()
 
     def blocks(count):
-        rows, cols = {2: (32, 1), 6: (32, 1), 24: (64, 2)}.get(count, (64, 1))
+        rows, cols = {1: (16, 1), 2: (32, 1), 6: (32, 1), 24: (64, 2)}.get(count, (64, 1))
         groups = count * ROWS // (rows * cols)
         if count == 48:
             return N.at[0, :, 0:3]
@@ -152,26 +152,55 @@
         return dev(dx=step) if p == phase else dev(dz=step)
 
     units = [(N, 0), (C, 0), (N, 1), (C, 1)]
-    ag = {}
-
-    def ag_own(u, phase):
+
+    def ag_block(u, phase, yh, off=0):
         ref, k = units[u]
-        where = (ag_first, ag_second)[phase]
+        for p in (0, 1):
+            for d, step in enumerate((1, -1)):
+                block = ag_first(ref, k, p, off, yh)
+                recv = ag_f.at[u, phase, p, d] if yh == d else ag_r.at[u, phase, 0]
+                begin(block, block, ag_s.at[u, phase], recv, ag_dev(p, phase, step))
+
+    def ag_early(a):
+        for k in (0, 1):
+            for yh in (0, 1):
+
+                @pl.when(jnp.logical_and(y_lo == k, y_hi == yh))
+                def _():
+                    ag_block(a + 2 * k, 0, yh)
+                    if k == 0:
+                        ag_block(a, 1, yh)
+
+    def ag_start(u):
+        k = units[u][1]
+        for yh in (0, 1):
+
+            @pl.when(jnp.logical_or(y_lo != k, y_hi != yh))
+            def _():
+                ag_block(u, 0, yh)
+                if k == 0:
+                    ag_block(u, 1, yh)
+
+    def ag_piece(u, offs):
+        for off in offs:
+            for yh in (0, 1):
+                ag_block(u, 1, yh, off)
+
+    def ag_own(u):
+        ref, k = units[u]
         for first in (0, 1):
             for p in (0, 1):
                 for d, step in enumerate((1, -1)):
-                    block = where(ref, k, p, 0, d if first == 0 else 1 - d)
-                    recv = ag_f.at[u, phase, p, d] if first == 0 else ag_r.at[u, phase, 0]
-                    cp = begin(block, block, ag_s.at[u, phase], recv, ag_dev(p, phase, step))
-                    if first == 0:
-                        ag[u, phase, p, d] = cp
+                    block = ag_second(ref, k, p, 0, d if first == 0 else 1 - d)
+                    recv = ag_f.at[u, 1, p, d] if first == 0 else ag_r.at[u, 1, 0]
+                    begin(block, block, ag_s.at[u, 1], recv, ag_dev(p, 1, step))
 
     def ag_fwd(u, phase):
         ref, k = units[u]
         where = (ag_first, ag_second)[phase]
         for p in (0, 1):
             for d, step in enumerate((1, -1)):
-                ag[u, phase, p, d].wait_recv()
+                take(ag_f.at[u, phase, p, d], blocks((1, 4)[phase]))
                 block = where(ref, k, p, -step, d)
                 begin(block, block, ag_s.at[u, phase], ag_r.at[u, phase, 1], ag_dev(p, phase, step))
 
@@ -196,14 +225,14 @@
     def partial_in(k):
         other = 1 - y_hi
 
-        @pl.loop(0, W_IN // TILE)
+        @pl.loop(0, W_IN // TILE, unroll=3)
         def _(j):
             cols = pl.ds(pl.multiple_of(j * TILE, TILE), TILE)
             XS[k, :, cols] = dot(rows_of(N, k, other), win[:, cols], ((1,), (0,))).astype(BF16)
 
         cp = send(XS.at[k, :, pl.ds(0, W_IN)], XR.at[k, :, pl.ds(0, W_IN)], e_s.at[k, 0], e_r.at[k, 0], partner)
 
-        @pl.loop(0, W_IN // TILE)
+        @pl.loop(0, W_IN // TILE, unroll=3)
         def _(j):
             cols = pl.ds(pl.multiple_of(j * TILE, TILE), TILE)
             H[k, :, cols] = dot(rows_of(N, k, y_hi), win[:, cols], ((1,), (0,)))
@@ -213,7 +242,7 @@
     def partial_out(k):
         other = 1 - y_hi
 
-        @pl.loop(0, W_OUT // TILE)
+        @pl.loop(0, W_OUT // TILE, unroll=2)
         def _(j):
             rows = pl.ds(pl.multiple_of(j * TILE, TILE), TILE)
             cols = pl.ds(pl.multiple_of(W_IN + j * TILE, TILE), TILE)
@@ -222,7 +251,7 @@
         cp = send(XS.at[k, :, pl.ds(W_IN, W_OUT)], XR.at[k, :, pl.ds(W_IN, W_OUT)],
                   e_s.at[k, 1], e_r.at[k, 1], partner)
 
-        @pl.loop(0, W_OUT // TILE)
+        @pl.loop(0, W_OUT // TILE, unroll=2)
         def _(j):
             rows = pl.ds(pl.multiple_of(j * TILE, TILE), TILE)
             cols = pl.ds(pl.multiple_of(W_IN + j * TILE, TILE), TILE)
@@ -284,7 +313,7 @@
         return send(ACT.at[k, y_hi], ACT.at[k, y_hi], e_s.at[k, 3], e_r.at[k, 3], partner)
 
     def normed_grad(k, yh):
-        @pl.loop(0, HALF // WIDE)
+        @pl.loop(0, HALF // WIDE, unroll=2)
         def _(j):
             cols = pl.ds(pl.multiple_of(j * WIDE, WIDE), WIDE)
             ng = dot(HG[k, yh], win[cols, :], ((1,), (1,)))
@@ -371,7 +400,7 @@
         dup_ref[tile_rows(t), :] = total[:, 3 * HEAD :].astype(BF16)
 
     def in_first(lo, hi):
-        @pl.loop(lo, hi)
+        @pl.loop(lo, hi, unroll=3)
         def _(t):
             SD[t] = grad_in(t, 1 - core, 0).astype(BF16)
             keep_in(t, grad_in(t, core, 0))
@@ -381,7 +410,7 @@
         ddown_ref[:, tile_rows(t)] = total[HEAD:].astype(BF16)
 
     def out_first():
-        @pl.loop(0, tiles)
+        @pl.loop(0, tiles, unroll=3)
         def _(t):
             SO[t] = grad_out(t, 1 - core, y_hi).astype(BF16)
             keep_out(t, grad_out(t, core, y_hi))
@@ -453,41 +482,45 @@
     stores = [pltpu.make_async_copy(src, dst, osem.at[i]) for i, (src, dst) in enumerate(results)]
 
     own, other = y_hi, 1 - y_hi
+    ag_early(0)
+    ag_early(1)
     y_wait(0, 0)
     y_start(1, 0)
-    ag_own(0, 0)
+    ag_start(0)
     y_wait(1, 0)
-    ag_own(1, 0)
+    ag_start(1)
     y_start(0, 1)
     y_start(1, 1)
     ag_fwd(0, 0)
-    ag_end(0, 0)
-    ag_own(0, 1)
+    ag_wait(0, 0, 1)
+    ag_piece(0, (1, -1))
+    ag_wait(0, 0, 2)
+    ag_piece(0, (2,))
     ag_fwd(1, 0)
     y_wait(0, 1)
-    ag_own(2, 0)
+    ag_start(2)
     ag_fwd(0, 1)
     ag_end(1, 0)
+    ag_piece(1, (1, -1, 2))
     ag_fwd(2, 0)
     for cp in loads:
         cp.wait()
+    y_wait(1, 1)
+    ag_start(3)
     ag_wait(0, 1, 1)
-    ag_own(1, 1)
-    y_wait(1, 1)
-    ag_own(3, 0)
     ag_end(0, 1)
     e_in0 = partial_in(0)
     ag_fwd(1, 1)
     ag_end(2, 0)
+    ag_own(2)
     ag_fwd(3, 0)
     ag_wait(1, 1, 1)
-    ag_own(2, 1)
     ag_end(1, 1)
     e_out0 = partial_out(0)
     ag_fwd(2, 1)
     ag_end(3, 0)
+    ag_own(3)
     ag_wait(2, 1, 1)
-    ag_own(3, 1)
     wait_all((e_in0, e_out0))
     back0 = middle(0)
     normed_grad(0, own)
@@ -529,27 +562,27 @@
     GC[core, 24:32, :] = GQ[...]
     gain_send(0, GC, core, [dev(dc=1)])
     in_away(0, 6)
+    gain_wait(0)
+    GY[y] = GC[0] + GC[1]
+    gain_send(1, GY, y, [dev(dy=d) for d in (1, 2, 3)])
     rs_mid(1, 1, other)
     rs_end(0, 0, own)
     rs_end(0, 0, other)
     to_owner(0)
-    gain_wait(0)
-    GY[y] = GC[0] + GC[1]
-    gain_send(1, GY, y, [dev(dy=d) for d in (1, 2, 3)])
     rs_end(1, 1, own)
     rs_start(1, 0, own)
-    in_here(0, 4)
+    in_here(0, 3)
     rs_end(1, 1, other)
     rs_start(1, 0, other)
-    in_here(4, 6)
+    in_here(3, 6)
     for cp in stores[:2]:
         cp.start()
-    rs_mid(1, 0, own)
-    rs_mid(1, 0, other)
     gain_wait(1)
     GX[x, 0] = GY[0] + GY[1]
     GX[x, 1] = GY[2] + GY[3]
     gain_send(2, GX, x, [dev(dx=d) for d in (1, 2, 3)])
+    rs_mid(1, 0, own)
+    rs_mid(1, 0, other)
     wait_all(acts)
     out_away(0, 6)
     rs_end(1, 0, own)

time: 138 us -> 130 us (0.942); the launches traced: 136 us -> 130 us
  Pallas kernels: 135 us -> 129 us
    pallas_call x1, Pallas kernels: 130 us -> 124 us  [per_device(): pl.pallas_call(kernel, name='block', out_shape=(jax.ShapeDtypeStruct((ROW...]
where the time goes in v4:
time: 130 us
  Pallas kernels  129 us (99%)
    pallas_call x1, Pallas kernels, per_device(): pl.pallas_call(kernel, name='block', out_shape=(jax.ShapeDtypeStruct((ROW...  124 us
    pallas_call x1, Pallas kernels, finish(): pl.pallas_call(widen, name='widen', grid=(steps,), in_specs=specs, out_sp...  5.11 us

profile of v4, /device:TPU:10, one launch (start us, length us, event | category | flops | bytes accessed | tf_op | source)
XLA Modules:
  0.0 130.0 jit_solution(2524105156215881167)
XLA Ops:
  0.6 124.2 %block.1 = (bf16[16,6144]{1,0:T(8,128)(2,1)}, f32[48,128]{1,0:T(8,128)}, f32[2,128]{1,0:T(2,128)}, bf16[3,1536,128]{2,1,0:T(8,128)(2,1)}, bf16[1536,384]{1,0:T(8...) custom-call(bf16[16,6144]{1,0:T(8,128)(2,1)} %tok_ref.1, bf16[16,6144]{1,0:T(8,128)(2,1)} %og_ref.1, ...), custom_call_target="tpu_custom_call" | custom-call | flops 20999999488 | bytes 20000000 | tf_op jit(solution)/shard_map/block/pallas_call | solution.py:690
  124.8 5.1 %widen.1 = (bf16[16,6144]{1,0:T(8,128)(2,1)}, f32[48,128]{1,0:T(8,128)}, f32[2,128]{1,0:T(2,128)}, f32[3,1536,128]{2,1,0:T(8,128)}, f32[1536,384]{1,0:T(8,128)},...) custom-call(bf16[16,6144]{1,0:T(8,128)(2,1)} %get-tuple-element.21.tg_ref, f32[48,128]{1,0:T(8,128)} %get-tuple-element.22.gain_ref, ...), custom_call_target="tpu_custom_call" | custom-call | tf_op jit(solution)/shard_map/widen/pallas_call | solution.py:742

commit v5 on v4

--- a/solution.py
+++ b/solution.py
@@ -30,9 +30,9 @@
 
 
 def kernel(
-    tok_ref, og_ref, gain_ref, gain_rows_ref, qg_ref, kg_ref, wqkv_ref, wup_ref, wproj_ref, wdown_ref,
+    tok_in, og_in, gain_in, gain_rows_in, qg_in, kg_in, wqkv_ref, wup_ref, wproj_ref, wdown_ref,
     tg_ref, gsum_ref, qk_ref, dqkv_hbm, dup_hbm, dproj_hbm, ddown_hbm,
-    nrm, N, C, G, win, wout, XS, XR, H, HG, ACT, FB1, MB1, FB2, MB2, FS, MS, YR,
+    tok_ref, og_ref, gain_ref, gain_rows_ref, qg_ref, kg_ref, isem, nrm, N, C, G, win, wout, XS, XR, H, HG, ACT, FB1, MB1, FB2, MB2, FS, MS, YR,
     SD, RD, SO, RO, GS, GQ, GC, GY, GX, GZ,
     dqkv_ref, dup_ref, dproj_ref, ddown_ref, osem, wsem, y_s, y_r, ag_s, ag_f, ag_r, e_s, e_r, rs_s, rs_f, rs_r, z_s, z_r, d_s, d_r, g_s, g_r,
 ):
@@ -77,6 +77,20 @@
         cp.start()
         pending.append(cp)
         return cp
+
+    barrier = pltpu.get_barrier_semaphore()
+    peers = [dev(dy=d) for d in (1, 2, 3)] + [dev(dx=d) for d in (1, 2, 3)]
+    peers += [dev(dz=d) for d in (1, 2, 3)] + [dev(dc=1)]
+    for peer in peers:
+        pl.semaphore_signal(barrier, inc=1, device_id=peer, device_id_type=MESH)
+
+    zrow = pl.ds(pl.multiple_of(z * ROWS, ROWS), ROWS)
+
+    inputs = ((tok_in, tok_ref), (gain_in, gain_ref), (og_in, og_ref), (gain_rows_in, gain_rows_ref), (qg_in, qg_ref),
+              (kg_in, kg_ref))
+    reads = [pltpu.make_async_copy(src, dst, isem.at[i]) for i, (src, dst) in enumerate(inputs)]
+    for cp in reads:
+        cp.start()
 
     half = pl.ds(pl.multiple_of(y_hi * HALF, HALF), HALF)
     loads = [
@@ -89,14 +103,9 @@
     for cp in loads:
         cp.start()
 
-    barrier = pltpu.get_barrier_semaphore()
-    peers = [dev(dy=d) for d in (1, 2, 3)] + [dev(dx=d) for d in (1, 2, 3)]
-    peers += [dev(dz=d) for d in (1, 2, 3)] + [dev(dc=1)]
-    for peer in peers:
-        pl.semaphore_signal(barrier, inc=1, device_id=peer, device_id_type=MESH)
-
-    zrow = pl.ds(pl.multiple_of(z * ROWS, ROWS), ROWS)
-
+
+    for cp in reads:
+        cp.wait()
     tok = tok_ref[...].astype(F32)
     scale = lax.rsqrt(jnp.mean(tok * tok, axis=1, keepdims=True) + EPS)
     nrm[...] = (tok * scale * gain_ref[...]).astype(BF16)
@@ -637,6 +646,13 @@
     dma = pltpu.SemaphoreType.DMA
     scratch = [
         pltpu.VMEM((ROWS, D), BF16),
+        pltpu.VMEM((ROWS, D), BF16),
+        pltpu.VMEM((1, D), F32),
+        pltpu.VMEM((D // HEAD, HEAD), F32),
+        pltpu.VMEM((1, HEAD), F32),
+        pltpu.VMEM((1, HEAD), F32),
+        dma((6,)),
+        pltpu.VMEM((ROWS, D), BF16),
         pltpu.VMEM((2, 2, 4, 64, HALF), BF16),
         pltpu.VMEM((2, 2, 4, 64, HALF), BF16),
         pltpu.VMEM((2, 2, 4, 64, HALF), BF16),
@@ -699,7 +715,7 @@
             jax.ShapeDtypeStruct((HEAD, QUART), BF16),
             jax.ShapeDtypeStruct((UP, QUART), BF16),
         ),
-        in_specs=[vm] * 6 + [hbm] * 4,
+        in_specs=[hbm] * 10,
         out_specs=(vm,) * 3 + (hbm,) * 4,
         scratch_shapes=scratch,
         compiler_params=pltpu.CompilerParams(

time: 130 us -> 131 us (level); the launches traced: 130 us -> 129 us
  no operation moved by 1% of the time
where the time goes in v5:
time: 131 us; the launch traced here: 129 us
  Pallas kernels  128 us (98%)
    pallas_call x1, Pallas kernels, per_device(): pl.pallas_call(kernel, name='block', out_shape=(jax.ShapeDtypeStruct((ROW...  123 us
    pallas_call x1, Pallas kernels, finish(): pl.pallas_call(widen, name='widen', grid=(steps,), in_specs=specs, out_sp...  5.11 us

profile of v5, /device:TPU:10, one launch (start us, length us, event | category | flops | bytes accessed | tf_op | source)
XLA Modules:
  0.0 129.1 jit_solution(7713995381433299079)
XLA Ops:
  0.6 123.3 %block.1 = (bf16[16,6144]{1,0:T(8,128)(2,1)}, f32[48,128]{1,0:T(8,128)}, f32[2,128]{1,0:T(2,128)}, bf16[3,1536,128]{2,1,0:T(8,128)(2,1)}, bf16[1536,384]{1,0:T(8...) custom-call(bf16[16,6144]{1,0:T(8,128)(2,1)} %tok_in.1, bf16[16,6144]{1,0:T(8,128)(2,1)} %og_in.1, ...), custom_call_target="tpu_custom_call" | custom-call | flops 20999999488 | bytes 20000000 | tf_op jit(solution)/shard_map/block/pallas_call | solution.py:706
  123.9 5.1 %widen.1 = (bf16[16,6144]{1,0:T(8,128)(2,1)}, f32[48,128]{1,0:T(8,128)}, f32[2,128]{1,0:T(2,128)}, f32[3,1536,128]{2,1,0:T(8,128)}, f32[1536,384]{1,0:T(8,128)},...) custom-call(bf16[16,6144]{1,0:T(8,128)(2,1)} %get-tuple-element.21.tg_ref, f32[48,128]{1,0:T(8,128)} %get-tuple-element.22.gain_ref, ...), custom_call_target="tpu_custom_call" | custom-call | tf_op jit(solution)/shard_map/widen/pallas_call | solution.py:758
